TPU v7x, 256 devices: a whole 4x4x8 slice. The times are simulated.
256 devices in a mesh: patch: 64 (over x, y_hi, z), head: 4 (over y_lo, core).
Axes of the slice: x: 4, y: 4 (y_hi: 2, y_lo: 2; y = y_hi * 2 + y_lo), z: 8, core: 2. Of those that a mesh axis runs over, the one named last changes fastest.
Arguments:
- image_tokens: bfloat16 [16384, 3072], P('patch'), may hold values from -6 to 6
- refresh: int32 [128], P('patch'), may hold values 0 or 1
- qkv_weight: bfloat16 [3072, 3, 1536], P(None, None, 'head'), may hold values from -0.109375 to 0.109375
- norm_gain: float32 [2, 128], replicated, may hold values from 1.2 to 2.2
- stale_kv: bfloat16 [16384, 2, 1536], P('patch', None, 'head'), may hold values from -4.5 to 4.5
- out_weight: bfloat16 [1536, 3072], P('head'), may hold values from -0.15625 to 0.15625
- stale_out: bfloat16 [16384, 3072], P('patch', 'head'), may hold values from -0.59765625 to 0.59765625
Outputs:
- layer_out: bfloat16 [16384, 3072], P('patch', 'head')
Inputs may be any that keep to these rules, and one draw needn't show every extreme that they name: `refresh`: 1 marks a tile whose keys, values and output are recomputed; 0 one served by the previous step.
All inputs are finite; a program needn't handle non-finite values. No bound on the sum of `refresh` on one device may be relied on, other than what follows from the above.
Results may differ from a plain program's by a relative error of at most 0.015.
Values may be sent and summed in bfloat16 or wider, within the bound.
A program may use at most 128 MiB of HBM per device.

v0:
```python
import math

import jax
import jax.numpy as jnp
from jax import lax
from jax.sharding import PartitionSpec as P


def rms_scale(values_in, gain_row):
    mean_square = jnp.mean(values_in * values_in, axis=-1, keepdims=True)
    return values_in * lax.rsqrt(mean_square + 1e-06) * gain_row


def local(image_tokens, refresh, qkv_weight, norm_gain, stale_kv, out_weight, stale_out):
    tok_rows = image_tokens.shape[0]
    model_width = image_tokens.shape[1]
    group_width = qkv_weight.shape[2]
    head_width = norm_gain.shape[1]
    group_heads = group_width // head_width
    tile_rows = tok_rows // refresh.shape[0]
    score_scale = 1.0 / math.sqrt(head_width)
    fresh_proj = jnp.dot(
        image_tokens,
        qkv_weight.reshape(model_width, 3 * group_width),
        preferred_element_type=jnp.float32,
    )
    fresh_proj = fresh_proj.reshape(tok_rows, 3, group_heads, head_width)
    queries = rms_scale(fresh_proj[:, 0], norm_gain[0]).astype(jnp.bfloat16)
    key_new = (
        rms_scale(fresh_proj[:, 1], norm_gain[1])
        .astype(jnp.bfloat16)
        .reshape(tok_rows, group_width)
    )
    value_new = fresh_proj[:, 2].astype(jnp.bfloat16).reshape(tok_rows, group_width)
    marked = jnp.repeat(refresh, tile_rows) > 0
    current = jnp.where(marked[:, None, None], jnp.stack([key_new, value_new], axis=1), stale_kv)
    query_heads = jnp.transpose(queries, (1, 0, 2))
    start_pair = (
        jnp.zeros((group_heads, tok_rows, head_width), jnp.float32),
        jnp.zeros((group_heads, tok_rows), jnp.float32),
    )
    totals = start_pair
    received = lax.all_gather(current, "patch", axis=0, tiled=True)
    key_count = received.shape[0]
    block_len = key_count
    while block_len > 2048 and block_len % 2 == 0:
        block_len = block_len // 2
    key_blocks = received.reshape(key_count // block_len, block_len, 2, group_heads, head_width)

    def advance(acc_pair, key_block):
        scores = (
            jnp.einsum(
                "hqd,khd->hqk", query_heads, key_block[:, 0], preferred_element_type=jnp.float32
            )
            * score_scale
        )
        weights = jnp.exp(scores)
        numerator = acc_pair[0] + jnp.einsum(
            "hqk,khd->hqd",
            weights.astype(jnp.bfloat16),
            key_block[:, 1],
            preferred_element_type=jnp.float32,
        )
        return ((numerator, acc_pair[1] + jnp.sum(weights, axis=-1)), None)

    totals, _ = lax.scan(advance, totals, key_blocks)
    numerator, denominator = totals
    attended = jnp.transpose(numerator / denominator[:, :, None], (1, 0, 2))
    attended = attended.reshape(tok_rows, group_width).astype(jnp.bfloat16)
    projected = jnp.dot(attended, out_weight, preferred_element_type=jnp.float32)
    own_columns = lax.psum_scatter(
        projected.astype(jnp.bfloat16), "head", scatter_dimension=1, tiled=True
    )
    return jnp.where(marked[:, None], own_columns, stale_out)


def solution(mesh):
    placed = (
        P("patch", None),
        P("patch"),
        P(None, None, "head"),
        P(),
        P("patch", None, "head"),
        P("head", None),
        P("patch", "head"),
    )
    return jax.shard_map(
        local, mesh=mesh, in_specs=placed, out_specs=P("patch", "head"), check_vma=False
    )
```

profile of v0, /device:TPU:1, one launch (start us, length us, event | category | flops | bytes accessed | tf_op | source)
XLA Modules:
  0.0 437.7 jit_solution(1796520020804075115)
XLA Ops:
  6.5 10.4 %copy.14 = bf16[3072,3,384]{0,2,1:T(8,128)(2,1)} copy(bf16[3072,3,384]{2,0,1:T(8,128)(2,1)} %param.11) | data formatting | bytes 14155776 | tf_op args[2]
  17.0 5.6 %fusion.5 = f32[256,3,3,128]{0,3,2,1:T(8,128)S(1)} fusion(bf16[3,3,128,3072]{3,2,1,0:T(8,128)(2,1)} %bitcast.83, bf16[256,3072]{1,0:T(8,128)(2,1)} %param.9), kind=kOutput, calls=%fused_computation.13 | convolution fusion | flops 1811939328 | bytes 9830400 | tf_op jit(solution)/shard_map/dot_general | solution.py:22
  23.8 1.3 copy.15
  28.5 272.3 %all-gather.2.cloned.1.call-done = bf16[16384,2,384]{0,2,1:T(8,128)(2,1)} async-done(((bf16[256,2,384]{0,2,1:T(8,128)(2,1)}), bf16[16384,2,384]{0,2,1:T(8,128)(2,1)}) %all-gather.2.cloned.1.call-update) | async-done | bytes 25165840 | tf_op jit(solution)/shard_map/all_gather | solution.py:43
  300.8 26.8 %copy.21 = bf16[96,8,8,2048]{3,2,1,0:T(8,128)(2,1)} copy(bf16[96,8,8,2048]{3,1,2,0:T(8,128)(2,1)} %bitcast.82) | data formatting | bytes 50331648
  327.6 34.4 %copy.16 = bf16[8,2048,2,3,128]{4,1,3,2,0:T(8,128)(2,1)} copy(bf16[8,2048,2,3,128]{1,0,4,3,2:T(8,128)(2,1)} %bitcast.81) | data formatting | bytes 50331648
  362.0 38.9 %while.13 = (s32[]{:T(128)}, f32[3,256,128]{2,1,0:T(8,128)S(1)}, f32[3,256]{1,0:T(4,128)S(1)}, bf16[8,2048,2,3,128]{4,1,3,2,0:T(8,128)(2,1)}, bf16[3,256,128]{2,1,0:T(8,128)(2,1)S(1)}, /*index=5*/s32[]{:T(128)}, s32[]{:T(128)}) while((s32[]{:T(128)}, f32[3,256,128]{2,1,0:T(8,128)S(1)}, f32[3,256]{1,0:T(4,128)S(1)}, ...), condition=%wide.region_4.5_spmd.clone, body=%wide.region_2.4_spmd.clone.sunk | while | flops 811795200 | bytes 23015524 | solution.py:66
  362.0 2.1 dynamic-slice_bitcast_fusion.2
  365.2 1.6 fusion.18
  366.8 2.1 dynamic-slice_bitcast_fusion.2
  370.1 1.6 fusion.18
  371.7 2.1 dynamic-slice_bitcast_fusion.2
  373.8 1.2 bitcast_reduce_fusion.2
  374.9 1.6 fusion.18
  376.5 2.1 dynamic-slice_bitcast_fusion.2
  378.6 1.2 bitcast_reduce_fusion.2
  379.8 1.6 fusion.18
  381.4 2.1 dynamic-slice_bitcast_fusion.2
  383.5 1.2 bitcast_reduce_fusion.2
  384.7 1.6 fusion.18
  386.3 2.1 dynamic-slice_bitcast_fusion.2
  388.4 1.2 bitcast_reduce_fusion.2
  389.5 1.6 fusion.18
  391.1 2.1 dynamic-slice_bitcast_fusion.2
  393.2 1.2 bitcast_reduce_fusion.2
  394.4 1.6 fusion.18
  396.0 2.1 dynamic-slice_bitcast_fusion.2
  398.1 1.2 bitcast_reduce_fusion.2
  399.3 1.6 fusion.18
  401.1 2.2 convolution_convert_fusion
  403.3 25.8 %reduce-scatter.2.cloned.1.call-done = bf16[256,768]{1,0:T(8,128)(2,1)} async-done(((bf16[256,3072]{1,0:T(8,128)(2,1)}), bf16[256,768]{1,0:T(8,128)(2,1)}) %reduce-scatter.2.cloned.1.call-update) | async-done | bytes 393232 | tf_op jit(solution)/shard_map/reduce_scatter | solution.py:71
  429.1 1.8 broadcast_select_fusion
  (42 shorter events, 7.2 us)
Async XLA Ops:
  6.5 394.6 %copy-start = (bf16[384,3072]{1,0:T(8,128)(2,1)S(1)}, bf16[384,3072]{1,0:T(8,128)(2,1)}, u32[]{:S(2)}) copy-start(bf16[384,3072]{1,0:T(8,128)(2,1)} %param.14) | copy-start | bytes 7077892
  6.5 294.2 %all-gather.2.cloned.1.call-start = ((), (), s32[]{:S(2)}) async-start(), calls=%async_computation.1 | async-start | bytes 25559040 | tf_op jit(solution)/shard_map/all_gather | solution.py:43
  17.0 6.7 %copy-start.4 = (s32[2]{0:T(128)S(1)}, s32[2]{0:T(128)}, u32[]{:S(2)}) copy-start(s32[2]{0:T(128)} %param.10) | copy-start | bytes 28
  17.0 6.8 %copy-start.3 = (f32[2,128]{1,0:T(2,128)S(1)}, f32[2,128]{1,0:T(2,128)}, u32[]{:S(2)}) copy-start(f32[2,128]{1,0:T(2,128)} %param.12) | copy-start | bytes 3076
  22.5 1.1 copy-start.1
  26.1 402.9 %reduce-scatter.2.cloned.1.call-start = ((), (), s32[]{:S(2)}) async-start(), calls=%async_computation.2 | async-start | bytes 1966080 | tf_op jit(solution)/shard_map/reduce_scatter | solution.py:71
  401.0 28.0 %copy-start.2 = (bf16[256,768]{1,0:T(8,128)(2,1)S(1)}, bf16[256,768]{1,0:T(8,128)(2,1)}, u32[]{:S(2)}) copy-start(bf16[256,768]{1,0:T(8,128)(2,1)} %param.15) | copy-start | bytes 1179652
Sparse Core Ops, SparseCore 0:
  26.2 274.4 all-gather.1
  403.4 25.5 reduce-scatter.1
where the time goes:
time: 440 us; the launch traced here: 438 us
  waiting for transfers between devices  298 us (68%)
  local copies, waits for them, and re-layouts  91.2 us (21%)
  matrix products  29.5 us (7%)
  between operations  13.5 us (3%)
  other arithmetic  5.11 us (1%)
    all_gather x1, waiting for transfers between devices, local(): received = lax.all_gather(current, 'patch', axis=0, tiled=True)  272 us
    unnamed x15, local copies, waits for them, and re-layouts  74.1 us
    reduce_scatter x1, waiting for transfers between devices, local(): lax.psum_scatter(projected.astype(jnp.bfloat16), 'head', scatter_dimensio...  25.8 us
    squeeze x8, local copies, waits for them, and re-layouts, local(): totals, _ = lax.scan(advance, totals, key_blocks)  16.8 us
    dot_general x8, matrix products, advance(): jnp.einsum('hqk,khd->hqd', weights.astype(jnp.bfloat16), key_block[:, 1],...  12.5 us
    dot_general x8, matrix products, advance(): jnp.einsum('hqd,khd->hqk', query_heads, key_block[:, 0], preferred_elemen...  9.28 us
  transfers between devices with their start and end apart: 2, of which 2 were waited for; matrix products, arithmetic and copies ran while one was open for 1% of the time, Pallas kernels for 0%

commit v1 on v0

v1 whole, which is shorter than its diff:
```python
import functools
import math

import jax
import jax.numpy as jnp
from jax import lax
from jax.experimental import pallas as pl
from jax.experimental.pallas import tpu as pltpu
from jax.sharding import Mesh
from jax.sharding import PartitionSpec as P

SPLIT = ("x", "yh", "z", "yl", "core")


def rms_scale(values_in, gain_row):
    mean_square = jnp.mean(values_in * values_in, axis=-1, keepdims=True)
    return values_in * lax.rsqrt(mean_square + 1e-06) * gain_row


def attend_kernel(q_ref, kv_ref, num_ref, den_ref, acc_ref):
    step = pl.program_id(1)

    @pl.when(step == 0)
    def _():
        acc_ref[...] = jnp.zeros_like(acc_ref)

    rows = q_ref.shape[1]
    keys = kv_ref.shape[2]
    key_block = kv_ref[0, 0]
    value_block = jnp.concatenate(
        [kv_ref[0, 1], jnp.ones((keys, 128), jnp.bfloat16)], axis=1
    )

    def body(i, carry):
        span = pl.ds(pl.multiple_of(i * 256, 256), 256)
        scores = lax.dot_general(
            q_ref[0, span], key_block, (((1,), (1,)), ((), ())),
            preferred_element_type=jnp.float32,
        )
        weights = jnp.exp2(scores).astype(jnp.bfloat16)
        acc_ref[span] += jnp.dot(weights, value_block, preferred_element_type=jnp.float32)
        return carry

    lax.fori_loop(0, rows // 256, body, 0)

    @pl.when(step == pl.num_programs(1) - 1)
    def _():
        num_ref[0] = acc_ref[:, :128]
        den_ref[0] = acc_ref[:, 128:]


def attend(q, kv):
    heads, rows, width = q.shape
    keys = kv.shape[2]
    block = 1024
    return pl.pallas_call(
        attend_kernel,
        grid=(heads, keys // block),
        in_specs=[
            pl.BlockSpec((1, rows, width), lambda h, s: (h, 0, 0)),
            pl.BlockSpec((1, 2, block, width), lambda h, s: (h, 0, s, 0)),
        ],
        out_specs=[
            pl.BlockSpec((1, rows, width), lambda h, s: (h, 0, 0)),
            pl.BlockSpec((1, rows, width), lambda h, s: (h, 0, 0)),
        ],
        out_shape=[
            jax.ShapeDtypeStruct((heads, rows, width), jnp.float32),
            jax.ShapeDtypeStruct((heads, rows, width), jnp.float32),
        ],
        scratch_shapes=[pltpu.VMEM((rows, 2 * width), jnp.float32)],
    )(q, kv)


def swap(array):
    pairs = []
    for t in range(2):
        for low in range(2):
            for g in range(2):
                pairs.append((t * 4 + low * 2 + g, g * 4 + (1 - low) * 2 + t))
    return lax.ppermute(array, ("yh", "yl", "core"), pairs)


def local(image_tokens, refresh, qkv_weight, norm_gain, stale_kv, out_weight, stale_out):
    rows, model_width = image_tokens.shape
    group_width = qkv_weight.shape[2]
    width = norm_gain.shape[1]
    heads = group_width // width
    tile_rows = rows // refresh.shape[0]
    scale = math.log2(math.e) / math.sqrt(width)
    weight = jnp.transpose(qkv_weight, (1, 0, 2))
    marked = jnp.repeat(refresh, tile_rows) > 0
    fresh = [
        jnp.dot(image_tokens, weight[j], preferred_element_type=jnp.float32).reshape(rows, heads, width)
        for j in range(3)
    ]
    queries = rms_scale(fresh[0], norm_gain[0] * scale).astype(jnp.bfloat16)
    key_new = rms_scale(fresh[1], norm_gain[1]).astype(jnp.bfloat16)
    value_new = fresh[2].astype(jnp.bfloat16)
    stale = stale_kv.reshape(rows, 2, heads, width)
    pick = marked[:, None, None]
    current = jnp.stack(
        [queries, jnp.where(pick, key_new, stale[:, 0]), jnp.where(pick, value_new, stale[:, 1])]
    )
    current = swap(jnp.transpose(current, (2, 0, 1, 3)))
    q = lax.all_gather(current[:, 0], "x", axis=1, tiled=True)
    kv = lax.all_gather(current[:, 1:], ("z", "core"), axis=2, tiled=True)
    numerator, denominator = attend(q, kv)
    numerator = lax.psum_scatter(numerator.astype(jnp.bfloat16), "x", scatter_dimension=1, tiled=True)
    denominator = lax.psum_scatter(denominator[:, :, 0], "x", scatter_dimension=1, tiled=True)
    attended = (numerator.astype(jnp.float32) / denominator[:, :, None]).astype(jnp.bfloat16)
    attended = jnp.transpose(swap(attended), (1, 0, 2)).reshape(rows, group_width)
    projected = jnp.dot(attended, out_weight, preferred_element_type=jnp.float32)
    own_columns = lax.psum_scatter(
        projected.astype(jnp.bfloat16), ("yl", "core"), scatter_dimension=1, tiled=True
    )
    return jnp.where(marked[:, None], own_columns, stale_out)


def solution(mesh):
    split = Mesh(mesh.devices.reshape(4, 2, 8, 2, 2), SPLIT)
    patch, head = ("x", "yh", "z"), ("yl", "core")
    placed = (
        P(patch, None),
        P(patch),
        P(None, None, head),
        P(),
        P(patch, None, head),
        P(head, None),
        P(patch, head),
    )
    return jax.shard_map(
        local, mesh=split, in_specs=placed, out_specs=P(patch, head), check_vma=False
    )
```

time: 440 us -> 237 us (0.54)
  waiting for transfers between devices: 298 us -> 119 us
  local copies, waits for them, and re-layouts: 91.2 us -> 32.3 us
  Pallas kernels: 0 us -> 29.9 us
  matrix products: 29.5 us -> 12 us
  blocking collectives: 0 us -> 12.3 us
  starting transfers between devices: 0.04 us -> 8.52 us
    all_gather x1, waiting for transfers between devices: 272 us -> 36.7 us  [local(): kv = lax.all_gather(current[:, 1:], ('z', 'core'), axis=2, tiled=True)]
    unnamed x15 -> x9, local copies, waits for them, and re-layouts: 74.1 us -> 10.9 us
    pallas_call x0 -> x1, Pallas kernels: none -> 29.9 us  [attend(): pl.pallas_call(attend_kernel, grid=(heads, keys // block), in_specs=[pl.B...]
    reduce_scatter x1 -> x2, waiting for transfers between devices: 25.8 us -> 53.2 us  [the longest x1 26.9 us: local(): lax.psum_scatter(numerator.astype(jnp.bfloat16), 'x', scatter_dimension=1...]
    dot_general x0 -> x6, local copies, waits for them, and re-layouts: none -> 20.4 us  [local(): jnp.dot(image_tokens, weight[j], preferred_element_type=jnp.float32)]
    unnamed x2 -> x5, waiting for transfers between devices: 0.03 us -> 18.2 us
    dot_general x17 -> x3, matrix products: 27.3 us -> 9.81 us  [local(): jnp.dot(image_tokens, weight[j], preferred_element_type=jnp.float32)]
    squeeze x8 -> x0, local copies, waits for them, and re-layouts: 16.8 us -> none  [local(): totals, _ = lax.scan(advance, totals, key_blocks)]
  transfers between devices with their start and end apart: 2 -> 6, of which waited for: 2 -> 6; matrix products, arithmetic and copies ran while one was open for 1% -> 1% of each run, Pallas kernels for 0% -> 0%
where the time goes in v1:
time: 237 us; the launch traced here: 236 us
  waiting for transfers between devices  119 us (50%)
  local copies, waits for them, and re-layouts  32.3 us (14%)
  Pallas kernels  29.9 us (13%)
  between operations  13.3 us (6%)
  blocking collectives  12.3 us (5%)
  matrix products  12 us (5%)
  other arithmetic  8.63 us (4%)
  starting transfers between devices  8.52 us (4%)
    all_gather x1, waiting for transfers between devices, local(): kv = lax.all_gather(current[:, 1:], ('z', 'core'), axis=2, tiled=True)  36.7 us
    pallas_call x1, Pallas kernels, attend(): pl.pallas_call(attend_kernel, grid=(heads, keys // block), in_specs=[pl.B...  29.9 us
    reduce_scatter x1, waiting for transfers between devices, local(): lax.psum_scatter(numerator.astype(jnp.bfloat16), 'x', scatter_dimension=1...  26.9 us
    reduce_scatter x1, waiting for transfers between devices, local(): lax.psum_scatter(projected.astype(jnp.bfloat16), ('yl', 'core'), scatter_...  26.3 us
    dot_general x6, local copies, waits for them, and re-layouts, local(): jnp.dot(image_tokens, weight[j], preferred_element_type=jnp.float32)  20.4 us
    unnamed x5, waiting for transfers between devices  18.2 us
    all_gather x1, blocking collectives, local(): q = lax.all_gather(current[:, 0], 'x', axis=1, tiled=True)  12.3 us
    ppermute x2, waiting for transfers between devices, swap(): return lax.ppermute(array, ('yh', 'yl', 'core'), pairs)  10.9 us
  transfers between devices with their start and end apart: 6, of which 6 were waited for; matrix products, arithmetic and copies ran while one was open for 1% of the time, Pallas kernels for 0%

profile of v1, /device:TPU:1, one launch (start us, length us, event | category | flops | bytes accessed | tf_op | source)
XLA Modules:
  0.0 235.9 jit_solution(1886204114925594256)
XLA Ops:
  6.5 0.8 broadcast_compare_fusion
  7.4 1.3 multiply_bitcast_fusion
  8.8 1.3 copy.28
  10.1 0.2 copy.37
  10.3 0.2 copy.38
  10.4 6.2 %slice_bitcast_fusion.2 = (bf16[384,3072]{0,1:T(8,128)(2,1)}, bf16[384,3072]{0,1:T(8,128)(2,1)}, bf16[384,3072]{0,1:T(8,128)(2,1)}) fusion(bf16[3,3072,384]{2,1,0:T(8,128)(2,1)} %bitcast.67), kind=kLoop, calls=%fused_computation.3 | loop fusion | bytes 14155776 | tf_op jit(solution)/shard_map/dot_general | solution.py:94
  16.6 4.3 %copy.24 = bf16[384,3072]{1,0:T(8,128)(2,1)} copy(bf16[384,3072]{0,1:T(8,128)(2,1)} %get-tuple-element.9) | data formatting | bytes 4718592 | tf_op jit(solution)/shard_map/dot_general | solution.py:94
  21.0 3.0 %multiply_reduce_fusion.1 = (f32[256,3]{0,1:T(4,128)S(1)}, f32[256,3,128]{0,2,1:T(8,128)S(1)}) fusion(bf16[3,128,3072]{2,1,0:T(8,128)(2,1)} %bitcast.70, bf16[256,3072]{1,0:T(8,128)(2,1)} %param.7), kind=kOutput, calls=%fused_computation.18 | convolution fusion | flops 604175616 | bytes 4328448 | tf_op jit(solution)/shard_map/dot_general | solution.py:94
  24.1 4.3 %copy.30 = bf16[384,3072]{1,0:T(8,128)(2,1)} copy(bf16[384,3072]{0,1:T(8,128)(2,1)} %get-tuple-element.10) | data formatting | bytes 4718592 | tf_op jit(solution)/shard_map/dot_general | solution.py:94
  28.4 4.3 %copy.26 = bf16[384,3072]{1,0:T(8,128)(2,1)} copy(bf16[384,3072]{0,1:T(8,128)(2,1)} %get-tuple-element.11) | data formatting | bytes 4718592 | tf_op jit(solution)/shard_map/dot_general | solution.py:94
  32.7 3.7 %multiply_reduce_fusion = (f32[256,3]{0,1:T(4,128)S(1)}, f32[256,3,128]{0,2,1:T(8,128)}) fusion(bf16[3,128,3072]{2,1,0:T(8,128)(2,1)} %bitcast.71, bf16[256,3072]{1,0:T(8,128)(2,1)} %param.7), kind=kOutput, calls=%fused_computation.16 | convolution fusion | flops 604175616 | bytes 4328448 | tf_op jit(solution)/shard_map/dot_general | solution.py:94
  36.4 1.2 copy.27
  37.6 0.9 fusion.15
  38.4 3.1 %fusion.12 = bf16[1,256,3,128]{3,1,0,2:T(8,128)(2,1)S(1)} fusion(bf16[3,128,3072]{2,1,0:T(8,128)(2,1)} %bitcast.69, bf16[256,3072]{1,0:T(8,128)(2,1)} %param.7, bf16[256,1,3,128]{3,0,2,1:T(8,128)(2,1)S(1)} %copy.38, pred[256]{0:T(512)(128)(4,1)S(1)} %broadcast_bitcast_fusion), kind=kOutput, calls=%fused_computation.12 | convolution fusion | flops 604176384 | bytes 4325632 | tf_op jit(solution)/shard_map/dot_general | solution.py:94
  41.6 0.2 fusion.17
  41.9 4.2 %collective-permute-start = (bf16[3,3,256,128]{3,2,1,0:T(8,128)(2,1)S(1)}, bf16[3,3,256,128]{3,2,1,0:T(8,128)(2,1)S(1)}, u32[]{:S(2)}, u32[]{:S(2)}) collective-permute-start(bf16[3,3,256,128]{3,2,1,0:T(8,128)(2,1)S(1)} %maximum_bitcast_fusion), channel_id=1, source_target_pairs={{0,2},{1,34},{2,0},{3,32},{32,3},{33,35},{34,1},{35,33},{4,6},{5,3... | collective-permute-start | bytes 1769480 | tf_op jit(solution)/shard_map/ppermute | solution.py:81
  46.1 7.6 %collective-permute-done = bf16[3,3,256,128]{3,2,1,0:T(8,128)(2,1)S(1)} collective-permute-done((bf16[3,3,256,128]{3,2,1,0:T(8,128)(2,1)S(1)}, bf16[3,3,256,128]{3,2,1,0:T(8,128)(2,1)S(1)}, u32[]{:S(2)}, u32[]{:S(2)}) %collective-permute-start) | collective-permute-done | bytes 589856 | tf_op jit(solution)/shard_map/ppermute | solution.py:81
  53.6 0.8 slice.46
  54.5 12.3 %all-gather = bf16[3,1,1024,128]{3,2,1,0:T(8,128)(2,1)} all-gather(bf16[3,1,256,128]{3,2,1,0:T(8,128)(2,1)S(1)} %slice.45), channel_id=2, replica_groups=mesh['x'=4,'yh'=2,'z'=8,'yl'=2,'core'=2] {'x'}, dimensions={2}, use_global_device_ids=true | all-gather | bytes 983040 | tf_op jit(solution)/shard_map/all_gather | solution.py:106
  66.8 36.7 %all-gather.3.cloned.1.call-done.kv_ref = bf16[3,2,4096,128]{3,2,1,0:T(8,128)(2,1)} async-done(((bf16[3,2,256,128]{3,2,1,0:T(8,128)(2,1)}), bf16[3,2,4096,128]{3,2,1,0:T(8,128)(2,1)}) %all-gather.3.cloned.1.call-update) | async-done | bytes 6291472 | tf_op jit(solution)/shard_map/all_gather | solution.py:107
  103.5 29.9 %shard_map.73 = (f32[3,1024,128]{2,1,0:T(8,128)}, f32[3,1024,128]{2,1,0:T(8,128)}) custom-call(bf16[3,1024,128]{2,1,0:T(8,128)(2,1)} %bitcast.68, bf16[3,2,4096,128]{3,2,1,0:T(8,128)(2,1)} %all-gather.3.cloned.1.call-done.kv_ref), custom_call_target="tpu_custom_call" | custom-call | tf_op jit(solution)/shard_map/pallas_call | solution.py:56
  133.4 8.2 %copy.36 = f32[3,1024,1]{0,1,2:T(8,128)} copy(f32[3,1024,1]{2,1,0:T(8,128)} %bitcast.74) | data formatting | bytes 24576
  141.7 2.4 %convert_element_type.24 = bf16[3,1024,128]{2,1,0:T(8,128)(2,1)} convert(f32[3,1024,128]{2,1,0:T(8,128)} %get-tuple-element.7) | non-fusion elementwise | flops 393216 | bytes 2359296 | tf_op jit(solution)/shard_map/convert_element_type | solution.py:109
  144.2 18.1 %reduce-scatter.10.cloned.1.call-done = f32[256,3]{1,0:T(8,128)} async-done(((f32[1024,3]{1,0:T(8,128)}), f32[256,3]{1,0:T(8,128)}) %reduce-scatter.10.cloned.1.call-update) | async-done | bytes 3088
  162.3 1.0 copy.35
  163.3 26.9 %reduce-scatter.6.cloned.1.call-done = bf16[3,256,128]{2,1,0:T(8,128)(2,1)} async-done(((bf16[3,1024,128]{2,1,0:T(8,128)(2,1)}), bf16[3,256,128]{2,1,0:T(8,128)(2,1)}) %reduce-scatter.6.cloned.1.call-update) | async-done | bytes 196624 | tf_op jit(solution)/shard_map/reduce_scatter | solution.py:109
  190.2 1.1 divide_convert_fusion
  191.3 4.2 %collective-permute-start.1 = (bf16[3,256,128]{2,1,0:T(8,128)(2,1)S(1)}, bf16[3,256,128]{2,1,0:T(8,128)(2,1)S(1)}, u32[]{:S(2)}, u32[]{:S(2)}) collective-permute-start(bf16[3,256,128]{2,1,0:T(8,128)(2,1)S(1)} %divide_convert_fusion), channel_id=1, source_target_pairs={{0,2},{1,34},{2,0},{3,32},{32,3},{33,35},{34,1},{35,33},{4,6},{5,3... | collective-permute-start | bytes 589832 | tf_op jit(solution)/shard_map/ppermute | solution.py:81
  195.5 3.4 %collective-permute-done.1 = bf16[3,256,128]{2,1,0:T(8,128)(2,1)S(1)} collective-permute-done((bf16[3,256,128]{2,1,0:T(8,128)(2,1)S(1)}, bf16[3,256,128]{2,1,0:T(8,128)(2,1)S(1)}, u32[]{:S(2)}, u32[]{:S(2)}) %collective-permute-start.1) | collective-permute-done | bytes 196640 | tf_op jit(solution)/shard_map/ppermute | solution.py:81
  199.0 2.2 convolution_convert_fusion
  201.2 26.3 %reduce-scatter.8.cloned.1.call-done = bf16[256,768]{1,0:T(8,128)(2,1)} async-done(((bf16[256,3072]{1,0:T(8,128)(2,1)}), bf16[256,768]{1,0:T(8,128)(2,1)}) %reduce-scatter.8.cloned.1.call-update) | async-done | bytes 393232 | tf_op jit(solution)/shard_map/reduce_scatter | solution.py:114
  227.6 1.8 broadcast_select_fusion
  (20 shorter events, 0.7 us)
Async XLA Ops:
  6.5 192.5 %copy-start = (bf16[384,3072]{1,0:T(8,128)(2,1)S(1)}, bf16[384,3072]{1,0:T(8,128)(2,1)}, u32[]{:S(2)}) copy-start(bf16[384,3072]{1,0:T(8,128)(2,1)} %param.12) | copy-start | bytes 7077892
  6.5 97.0 %all-gather.3.cloned.1.call-start = ((), (), s32[]{:S(2)}) async-start(), calls=%async_computation.3 | async-start | bytes 6684672 | tf_op jit(solution)/shard_map/all_gather | solution.py:107
  41.9 11.8 %collective-permute-start = (bf16[3,3,256,128]{3,2,1,0:T(8,128)(2,1)S(1)}, bf16[3,3,256,128]{3,2,1,0:T(8,128)(2,1)S(1)}, u32[]{:S(2)}, u32[]{:S(2)}) collective-permute-start(bf16[3,3,256,128]{3,2,1,0:T(8,128)(2,1)S(1)} %maximum_bitcast_fusion), channel_id=1, source_target_pairs={{0,2},{1,34},{2,0},{3,32},{32,3},{33,35},{34,1},{35,33},{4,6},{5,3... | collective-permute-start | bytes 1769480 | tf_op jit(solution)/shard_map/ppermute | solution.py:81
  54.4 107.9 %reduce-scatter.10.cloned.1.call-start = ((), (), s32[]{:S(2)}) async-start(), calls=%async_computation.6 | async-start | bytes 655360
  141.7 48.5 %reduce-scatter.6.cloned.1.call-start = ((), (), s32[]{:S(2)}) async-start(), calls=%async_computation.4 | async-start | bytes 983040 | tf_op jit(solution)/shard_map/reduce_scatter | solution.py:109
  144.2 83.4 %reduce-scatter.8.cloned.1.call-start = ((), (), s32[]{:S(2)}) async-start(), calls=%async_computation.5 | async-start | bytes 1966080 | tf_op jit(solution)/shard_map/reduce_scatter | solution.py:114
  191.3 7.5 %collective-permute-start.1 = (bf16[3,256,128]{2,1,0:T(8,128)(2,1)S(1)}, bf16[3,256,128]{2,1,0:T(8,128)(2,1)S(1)}, u32[]{:S(2)}, u32[]{:S(2)}) collective-permute-start(bf16[3,256,128]{2,1,0:T(8,128)(2,1)S(1)} %divide_convert_fusion), channel_id=1, source_target_pairs={{0,2},{1,34},{2,0},{3,32},{32,3},{33,35},{34,1},{35,33},{4,6},{5,3... | collective-permute-start | bytes 589832 | tf_op jit(solution)/shard_map/ppermute | solution.py:81
  199.0 28.5 %copy-start.1 = (bf16[256,768]{1,0:T(8,128)(2,1)S(1)}, bf16[256,768]{1,0:T(8,128)(2,1)}, u32[]{:S(2)}) copy-start(bf16[256,768]{1,0:T(8,128)(2,1)} %param.13) | copy-start | bytes 1179652
Sparse Core Ops, SparseCore 0:
  54.6 48.8 all-gather.2
  141.8 20.4 reduce-scatter.9
  164.9 25.2 reduce-scatter.5
  201.3 26.1 reduce-scatter.7

commit v2 on v0

v2 whole, which is shorter than its diff:
```python
import functools
import math

import jax
import jax.numpy as jnp
from jax import lax
from jax.experimental import pallas as pl
from jax.experimental.pallas import tpu as pltpu
from jax.sharding import PartitionSpec as P

MESH = pl.DeviceIdType.MESH
ROWS_BY_ROWS = (((1,), (1,)), ((), ()))
COLUMNS_BY_COLUMNS = (((0,), (0,)), ((), ()))


def kernel(
    nx, nz,
    tokens, refresh, qkv_weight, gain, stale_kv, out_weight, stale_out,
    out,
    weight_buf, stage, kv_buf, q_buf, acc, den,
    num_stage, num_in, den_in, att_stage, att_all, out_weight_all,
    load_sem, own_sem,
    swap_s, swap_r, x_s, x_r, z_s, z_r, sib_s, sib_r, w_s, w_r, sum_s, sum_r, att_s, att_r,
):
    heads, _, rows, width = stage.shape
    half = nz // 2
    out_cols = stale_out.shape[1]
    tile_rows = rows // refresh.shape[0]
    patch, head = lax.axis_index("patch"), lax.axis_index("head")
    x, yh, z = patch // (2 * nz), (patch // nz) % 2, patch % nz
    yl, core = head // 2, head % 2

    def device(x_to, yh_to, z_to, yl_to, core_to):
        return ((x_to * 2 + yh_to) * nz + z_to, yl_to * 2 + core_to)

    sibling = device(x, yh, z, yl, 1 - core)
    swapped = device(x, core, z, 1 - yl, yh)
    along_z = (
        device(x, yh, (z + 1) % nz, yl, core),
        device(x, yh, (z + nz - 1) % nz, yl, core),
    )

    def along_x(step):
        return device((x + step) % nx, yh, z, yl, core)

    def send(src, dst, send_sem, recv_sem, to):
        return pltpu.make_async_remote_copy(
            src_ref=src, dst_ref=dst, send_sem=send_sem, recv_sem=recv_sem,
            device_id=to, device_id_type=MESH,
        )

    def load(h, j):
        return pltpu.make_async_copy(
            qkv_weight.at[j, :, pl.ds(pl.multiple_of(h * width, width), width)],
            weight_buf.at[h, :, pl.ds(j * width, width)],
            load_sem.at[h, j],
        )

    def swap_kv(h):
        return send(stage.at[h, pl.ds(1, 2)], kv_buf.at[h, :, 0], swap_s.at[h, 0], swap_r.at[h, 0], swapped)

    def swap_q(h):
        return send(stage.at[h, 0], q_buf.at[h, 0], swap_s.at[h, 1], swap_r.at[h, 1], swapped)

    def gather_x(h, j):
        return send(q_buf.at[h, 0], q_buf.at[h, j], x_s.at[h, j - 1], x_r.at[h, j - 1], along_x(j))

    def spot(s, way):
        return 0 if s == 0 else 4 * s - 2 + way

    def ring(h, s, way):
        if s < half - 1:
            src, dst = kv_buf.at[h, :, spot(s, way)], kv_buf.at[h, :, spot(s + 1, way)]
        else:
            src, dst = kv_buf.at[h, way, spot(s, way)], kv_buf.at[h, way, 4 * half - 2]
        return send(src, dst, z_s.at[h, s, way], z_r.at[h, s, way], along_z[way])

    def share(h, s, first, count):
        return send(
            kv_buf.at[h, :, pl.ds(first, count)], kv_buf.at[h, :, pl.ds(first + count, count)],
            sib_s.at[h, s], sib_r.at[h, s], sibling,
        )

    def share_own(h):
        return share(h, 0, 0, 1)

    def share_step(h, s):
        return share(h, s, 4 * s - 2, 2)

    def share_last(h):
        return share(h, half, 4 * half - 2, 1)

    group = yl * 2 + core
    cross_yh = (yh + core) % 2

    def weight_columns(block):
        return out_weight.at[:, :, pl.ds(pl.multiple_of(block * out_cols, out_cols), out_cols)]

    def weight_own():
        return pltpu.make_async_copy(weight_columns(group), out_weight_all.at[:, group], own_sem)

    def weight_sibling(slot):
        return send(
            weight_columns(yl * 2 + 1 - core), out_weight_all.at[:, slot],
            w_s.at[2], w_r.at[2], sibling,
        )

    def weight_cross(c, slot, source_core):
        return send(
            weight_columns((1 - yl) * 2 + c), out_weight_all.at[:, slot],
            w_s.at[c], w_r.at[source_core], device(x, cross_yh, z, 1 - yl, c),
        )

    def sum_num(h, j):
        return send(
            num_stage.at[h, j - 1], num_in.at[h, j - 1],
            sum_s.at[h, j - 1, 0], sum_r.at[h, j - 1, 0], along_x(nx - j),
        )

    def sum_den(h, j):
        return send(
            den.at[h, :, pl.ds(j * rows, rows)], den_in.at[h, j - 1],
            sum_s.at[h, j - 1, 1], sum_r.at[h, j - 1, 1], along_x(nx - j),
        )

    held_group = (1 - yl) * 2 + yh

    def hand_out(h, d, slot):
        return send(
            att_stage.at[h], att_all.at[h, slot],
            att_s.at[h, d], att_r.at[h, slot], device(x, core, z, d // 2, d % 2),
        )

    def compute(h, first, count, fresh):
        keys = kv_buf[h, 0, pl.ds(first, count)].reshape(count * rows, width)
        values = kv_buf[h, 1, pl.ds(first, count)].reshape(count * rows, width)
        scores = lax.dot_general(
            keys, q_buf[h].reshape(nx * rows, width), ROWS_BY_ROWS, preferred_element_type=jnp.float32
        )
        weights = jnp.exp2(scores)
        part = jnp.sum(weights.reshape(count * rows // 8, 8, nx * rows), axis=0)
        product = lax.dot_general(
            values, weights.astype(jnp.bfloat16), COLUMNS_BY_COLUMNS, preferred_element_type=jnp.float32
        )
        if fresh:
            acc[h], den[h] = product, part
        else:
            acc[h] += product
            den[h] += part

    def marked(i, shape):
        return jnp.broadcast_to(refresh[i], shape) > 0

    def normed(part, row):
        mean_square = jnp.mean(part * part, axis=-1, keepdims=True)
        return part * lax.rsqrt(mean_square + 1e-06) * row

    for h in range(heads):
        for j in range(3):
            load(h, j).start()

    barrier = pltpu.get_barrier_semaphore()
    peers = [along_x(j) for j in range(1, nx)] + list(along_z)
    for other in range(1, 8):
        bits = (other // 4, (other // 2) % 2, other % 2)
        peers.append(device(x, (yh + bits[0]) % 2, z, (yl + bits[1]) % 2, (core + bits[2]) % 2))
    for peer in peers:
        pl.semaphore_signal(barrier, inc=1, device_id=peer, device_id_type=MESH)
    pl.semaphore_wait(barrier, len(peers))

    scale = math.log2(math.e) / math.sqrt(width)
    query_gain = gain[pl.ds(0, 1), :] * scale
    key_gain = gain[pl.ds(1, 1), :]

    def project(h, carry):
        for j in range(3):
            load(h, j).wait()
        fresh = jnp.dot(tokens[...], weight_buf[h], preferred_element_type=jnp.float32)
        stage[h, 0] = normed(fresh[:, :width], query_gain).astype(jnp.bfloat16)
        current = (normed(fresh[:, width : 2 * width], key_gain), fresh[:, 2 * width :])
        for j in range(2):
            for i in range(refresh.shape[0]):
                span = slice(i * tile_rows, (i + 1) * tile_rows)
                stale = stale_kv[h, j, span].astype(jnp.float32)
                stage[h, 1 + j, span] = jnp.where(
                    marked(i, stale.shape), current[j][span], stale
                ).astype(jnp.bfloat16)
        swap_kv(h).start()
        swap_q(h).start()
        return carry

    lax.fori_loop(0, heads, project, 0)

    def distribute(h, carry):
        swap_kv(h).wait_recv()
        for way in range(2):
            ring(h, 0, way).start()
        share_own(h).start()
        swap_q(h).wait_recv()
        for j in range(1, nx):
            gather_x(h, j).start()
        return carry

    lax.fori_loop(0, heads, distribute, 0)
    weight_own().start()
    weight_sibling(group).start()
    for c in range(2):
        weight_cross(c, group, core).start()

    for s in range(1, half):

        def event(h, carry, s=s):
            for way in range(2):
                ring(h, s - 1, way).wait_recv()
            for way in range(2):
                ring(h, s, way).start()
            share_step(h, s).start()
            if s == 1:
                for j in range(1, nx):
                    gather_x(h, j).wait_recv()
                share_own(h).wait_recv()
                compute(h, 0, 2, True)

                @pl.when(h > 0)
                def _():
                    share_step(h - 1, 1).wait_recv()
                    compute(h - 1, 2, 4, False)
            else:
                late_h = (h + heads - 1) % heads
                late_s = s - jnp.where(h == 0, 1, 0)
                share_step(late_h, late_s).wait_recv()
                compute(late_h, 4 * late_s - 2, 4, False)
            return carry

        lax.fori_loop(0, heads, event, 0)

    share_step(heads - 1, half - 1).wait_recv()
    compute(heads - 1, 4 * half - 6, 4, False)

    def finish(h):
        share_last(h).wait_recv()
        compute(h, 4 * half - 2, 2, False)
        for j in range(1, nx):
            num_stage[h, j - 1] = acc[h, :, j * rows : (j + 1) * rows].astype(jnp.bfloat16)
            sum_num(h, j).start()
            sum_den(h, j).start()

    def last_event(h, carry):
        for way in range(2):
            ring(h, half - 1, way).wait_recv()
        share_last(h).start()

        @pl.when(h > 0)
        def _():
            finish(h - 1)

        return carry

    lax.fori_loop(0, heads, last_event, 0)
    finish(heads - 1)

    def attended(h, carry):
        numerator = acc[h, :, :rows]
        denominator = den[h, :, :rows]
        for j in range(1, nx):
            sum_num(h, j).wait_recv()
            sum_den(h, j).wait_recv()
            numerator += num_in[h, j - 1].astype(jnp.float32)
            denominator += den_in[h, j - 1]
        denominator = jnp.sum(denominator, axis=0, keepdims=True)
        result = (numerator / denominator).astype(jnp.bfloat16)
        att_stage[h] = result
        for d in range(4):

            @pl.when(jnp.logical_or(yh != core, head != d))
            def _(d=d):
                hand_out(h, d, held_group).start()

        @pl.when(yh == core)
        def _():
            att_all[h, held_group] = result

        return carry

    lax.fori_loop(0, heads, attended, 0)

    weight_own().wait()
    weight_sibling(yl * 2 + 1 - core).wait_recv()
    for source_core in range(2):
        weight_cross(0, (1 - yl) * 2 + source_core, source_core).wait_recv()
    total = None
    for h in range(heads):
        for slot in range(4):

            @pl.when(jnp.logical_or(yh != core, held_group != slot))
            def _(h=h, slot=slot):
                hand_out(h, 0, slot).wait_recv()

        part = lax.dot_general(
            att_all[h].reshape(4 * width, rows),
            out_weight_all[h].reshape(4 * width, out_cols),
            COLUMNS_BY_COLUMNS,
            preferred_element_type=jnp.float32,
        )
        total = part if total is None else total + part
    for i in range(refresh.shape[0]):
        span = slice(i * tile_rows, (i + 1) * tile_rows)
        stale = stale_out[span].astype(jnp.float32)
        out[span] = jnp.where(marked(i, stale.shape), total[span], stale).astype(jnp.bfloat16)

    weight_sibling(group).wait_send()
    for c in range(2):
        weight_cross(c, group, core).wait_send()

    def drain(h, carry):
        swap_kv(h).wait_send()
        swap_q(h).wait_send()
        for j in range(1, nx):
            gather_x(h, j).wait_send()
            sum_num(h, j).wait_send()
            sum_den(h, j).wait_send()
        for s in range(half):
            for way in range(2):
                ring(h, s, way).wait_send()
        share_own(h).wait_send()
        for s in range(1, half):
            share_step(h, s).wait_send()
        share_last(h).wait_send()
        for d in range(4):

            @pl.when(jnp.logical_or(yh != core, head != d))
            def _(d=d):
                hand_out(h, d, held_group).wait_send()

        return carry

    lax.fori_loop(0, heads, drain, 0)


def local(nx, nz, image_tokens, refresh, qkv_weight, norm_gain, stale_kv, out_weight, stale_out):
    rows, model_width = image_tokens.shape
    group_width = qkv_weight.shape[2]
    width = norm_gain.shape[1]
    heads = group_width // width
    half = nz // 2
    out_cols = stale_out.shape[1]
    weight = jnp.transpose(qkv_weight, (1, 0, 2))
    stale = jnp.transpose(stale_kv.reshape(rows, 2, heads, width), (2, 1, 0, 3))
    bf16, f32 = jnp.bfloat16, jnp.float32
    dma = pltpu.SemaphoreType.DMA
    vmem = pl.BlockSpec(memory_space=pltpu.VMEM)
    smem = pl.BlockSpec(memory_space=pltpu.SMEM)
    anywhere = pl.BlockSpec(memory_space=pl.ANY)
    return pl.pallas_call(
        functools.partial(kernel, nx, nz),
        out_shape=jax.ShapeDtypeStruct((rows, out_cols), bf16),
        in_specs=[vmem, smem, anywhere, vmem, vmem, anywhere, vmem],
        out_specs=vmem,
        scratch_shapes=[
            pltpu.VMEM((heads, model_width, 3 * width), bf16),
            pltpu.VMEM((heads, 3, rows, width), bf16),
            pltpu.VMEM((heads, 2, 4 * half, rows, width), bf16),
            pltpu.VMEM((heads, nx, rows, width), bf16),
            pltpu.VMEM((heads, width, nx * rows), f32),
            pltpu.VMEM((heads, 8, nx * rows), f32),
            pltpu.VMEM((heads, nx - 1, width, rows), bf16),
            pltpu.VMEM((heads, nx - 1, width, rows), bf16),
            pltpu.VMEM((heads, nx - 1, 8, rows), f32),
            pltpu.VMEM((heads, width, rows), bf16),
            pltpu.VMEM((heads, 4, width, rows), bf16),
            pltpu.VMEM((heads, 4, width, out_cols), bf16),
            dma((heads, 3)), dma,
            dma((heads, 2)), dma((heads, 2)),
            dma((heads, nx - 1)), dma((heads, nx - 1)),
            dma((heads, half, 2)), dma((heads, half, 2)),
            dma((heads, half + 1)), dma((heads, half + 1)),
            dma((3,)), dma((3,)),
            dma((heads, nx - 1, 2)), dma((heads, nx - 1, 2)),
            dma((heads, 4)), dma((heads, 4)),
        ],
        compiler_params=pltpu.CompilerParams(
            collective_id=0, has_side_effects=True, vmem_limit_bytes=50 << 20
        ),
    )(
        image_tokens, refresh, weight, norm_gain, stale,
        out_weight.reshape(heads, width, out_weight.shape[1]), stale_out,
    )


def solution(mesh, nx=4, nz=8):
    placed = (
        P("patch", None),
        P("patch"),
        P(None, None, "head"),
        P(),
        P("patch", None, "head"),
        P("head", None),
        P("patch", "head"),
    )
    return jax.shard_map(
        functools.partial(local, nx, nz),
        mesh=mesh, in_specs=placed, out_specs=P("patch", "head"), check_vma=False,
    )
```

time: 440 us -> 72.9 us (0.17)
  waiting for transfers between devices: 298 us -> 0 us
  local copies, waits for them, and re-layouts: 91.2 us -> 4.72 us
  Pallas kernels: 0 us -> 68 us
  matrix products: 29.5 us -> 0 us
  between operations: 13.5 us -> 0.04 us
  other arithmetic: 5.11 us -> 0 us
    all_gather x1 -> x0, waiting for transfers between devices: 272 us -> none  [local(): received = lax.all_gather(current, 'patch', axis=0, tiled=True)]
    unnamed x15 -> x10, local copies, waits for them, and re-layouts: 74.1 us -> 4.5 us
    pallas_call x0 -> x1, Pallas kernels: none -> 68 us  [local(): pl.pallas_call(functools.partial(kernel, nx, nz), out_shape=jax.ShapeDtyp...]
    dot_general x18 -> x0, matrix products: 29.5 us -> none  [the longest x8 12.5 us: advance(): jnp.einsum('hqk,khd->hqd', weights.astype(jnp.bfloat16), key_block[:, 1],...]
    reduce_scatter x1 -> x0, waiting for transfers between devices: 25.8 us -> none  [local(): lax.psum_scatter(projected.astype(jnp.bfloat16), 'head', scatter_dimensio...]
    squeeze x8 -> x0, local copies, waits for them, and re-layouts: 16.8 us -> none  [local(): totals, _ = lax.scan(advance, totals, key_blocks)]
  transfers between devices with their start and end apart: 2 -> 0, of which waited for: 2 -> 0; matrix products, arithmetic and copies ran while one was open for 1% -> 0% of each run, Pallas kernels for 0% -> 0%
where the time goes in v2:
time: 72.9 us; the launch traced here: 72.8 us
  Pallas kernels  68 us (93%)
  local copies, waits for them, and re-layouts  4.72 us (6%)
    pallas_call x1, Pallas kernels, local(): pl.pallas_call(functools.partial(kernel, nx, nz), out_shape=jax.ShapeDtyp...  68 us
    unnamed x10, local copies, waits for them, and re-layouts  4.5 us

profile of v2, /device:TPU:1, one launch (start us, length us, event | category | flops | bytes accessed | tf_op | source)
XLA Modules:
  0.0 72.8 jit_solution(3022800321899839285)
XLA Ops:
  0.0 0.0 copy-start
  0.0 1.4 %copy.8 = bf16[256,2,384]{0,2,1:T(8,128)(2,1)S(1)} copy(bf16[256,2,384]{2,1,0:T(2,128)(2,1)} %param.11) | data formatting | bytes 786432 | tf_op args[4]
  1.4 0.2 copy.9
  1.7 0.0 copy-done
  1.7 0.0 copy-start.1
  1.7 1.0 %copy-done.1 = bf16[256,768]{1,0:T(8,128)(2,1)S(1)} copy-done((bf16[256,768]{1,0:T(8,128)(2,1)S(1)}, bf16[256,768]{1,0:T(8,128)(2,1)}, u32[]{:S(2)}) %copy-start.1) | copy-done | bytes 393240
  2.7 0.0 copy-start.2
  2.7 0.7 copy-done.2
  3.3 0.0 copy-start.3
  3.4 0.7 copy-done.3
  4.0 68.0 %shard_map.73 = bf16[256,768]{1,0:T(8,128)(2,1)S(1)} custom-call(bf16[256,3072]{1,0:T(8,128)(2,1)S(1)} %copy-done, s32[2]{0:T(128)S(1)} %copy-done.3, bf16[3,3072,384]{2,1,0:T(8,128)(2,1)} %bitcast.5, f32[2,128]{1,0:T(2,128)S(1)} %copy-done.2, bf16[3,2,256,128]{3,2,1,0:T(8,128)(2,1)S(1)} %bitcast.4, bf16[3,128,3072]{2,1,0:T(8,128)(2,1)} %bitcast.6, ...), custom_call_target="tpu_custom_call" | custom-call | tf_op jit(solution)/shard_map/pallas_call | solution.py:354
  72.0 0.7 %copy.11 = bf16[256,768]{1,0:T(8,128)(2,1)} copy(bf16[256,768]{1,0:T(8,128)(2,1)S(1)} %shard_map.73) | data formatting | bytes 786432
Async XLA Ops:
  0.0 1.7 %copy-start = (bf16[256,3072]{1,0:T(8,128)(2,1)S(1)}, bf16[256,3072]{1,0:T(8,128)(2,1)}, u32[]{:S(2)}) copy-start(bf16[256,3072]{1,0:T(8,128)(2,1)} %tokens.1) | copy-start | bytes 4718596
  1.7 1.0 %copy-start.1 = (bf16[256,768]{1,0:T(8,128)(2,1)S(1)}, bf16[256,768]{1,0:T(8,128)(2,1)}, u32[]{:S(2)}) copy-start(bf16[256,768]{1,0:T(8,128)(2,1)} %stale_out.1) | copy-start | bytes 1179652
  2.7 0.7 copy-start.2
  3.3 0.7 copy-start.3

commit v3 on v2

v3 whole, which is shorter than its diff:
```python
import functools
import math

import jax
import jax.numpy as jnp
from jax import lax
from jax.experimental import pallas as pl
from jax.experimental.pallas import tpu as pltpu
from jax.sharding import PartitionSpec as P

MESH = pl.DeviceIdType.MESH
ROWS_BY_ROWS = (((1,), (1,)), ((), ()))
COLUMNS_BY_COLUMNS = (((0,), (0,)), ((), ()))


def kernel(
    nx, nz,
    tokens_far, refresh_far, qkv_weight, gain_far, stale_kv_far, out_weight, stale_out_far,
    out,
    tokens, refresh, gain, stale_kv, stale_out,
    kv_weight, q_weight, stage, kv_buf, q_buf, acc, den,
    num_stage, num_in, den_in, att_stage, att_all, out_weight_all,
    load_sem, own_sem,
    swap_s, swap_r, x_s, x_r, z_s, z_r, sib_s, sib_r, w_s, w_r, sum_s, sum_r, att_s, att_r,
):
    heads, _, rows, width = stage.shape
    half = nz // 2
    out_cols = stale_out.shape[1]
    tiles = refresh.shape[0]
    tile_rows = rows // tiles
    patch, head = lax.axis_index("patch"), lax.axis_index("head")
    x, yh, z = patch // (2 * nz), (patch // nz) % 2, patch % nz
    yl, core = head // 2, head % 2

    def device(x_to, yh_to, z_to, yl_to, core_to):
        return ((x_to * 2 + yh_to) * nz + z_to, yl_to * 2 + core_to)

    sibling = device(x, yh, z, yl, 1 - core)
    swapped = device(x, core, z, 1 - yl, yh)
    along_z = (
        device(x, yh, (z + 1) % nz, yl, core),
        device(x, yh, (z + nz - 1) % nz, yl, core),
    )

    def along_x(step):
        return device((x + step) % nx, yh, z, yl, core)

    def send(src, dst, send_sem, recv_sem, to):
        return pltpu.make_async_remote_copy(
            src_ref=src, dst_ref=dst, send_sem=send_sem, recv_sem=recv_sem,
            device_id=to, device_id_type=MESH,
        )

    def load_kv_weight(h, j):
        return pltpu.make_async_copy(
            qkv_weight.at[1 + j, :, pl.ds(h * width, width)],
            kv_weight.at[h, :, pl.ds(j * width, width)],
            load_sem.at[2 * h + j],
        )

    def load(far, near, index):
        return pltpu.make_async_copy(far, near, load_sem.at[2 * heads + index])

    load_tokens = load(tokens_far, tokens, 0)
    load_refresh = load(refresh_far, refresh, 1)
    load_gain = load(gain_far, gain, 2)
    load_stale_kv = load(stale_kv_far, stale_kv, 3)
    load_stale_out = load(stale_out_far, stale_out, 4)
    load_q_weight = load(qkv_weight.at[0], q_weight, 5)

    def swap(h, j):
        dst = q_buf.at[h, 0] if j == 0 else kv_buf.at[h, j - 1, 0]
        return send(stage.at[h, j], dst, swap_s.at[h, j], swap_r.at[h, j], swapped)

    def gather_x(h, j):
        return send(q_buf.at[h, 0], q_buf.at[h, j], x_s.at[h, j - 1], x_r.at[h, j - 1], along_x(j))

    def spot(s, way):
        return 4 * s - 2 + way

    def move(h, s, way, c, src, dst):
        return send(src, dst, z_s.at[h, s, way, c], z_r.at[h, s, way, c], along_z[way])

    def ring_own(h, way, c):
        return move(h, 0, way, c, kv_buf.at[h, c, 0], kv_buf.at[h, c, spot(1, way)])

    def ring(h, s, way, c):
        return move(h, s, way, c, kv_buf.at[h, c, spot(s, way)], kv_buf.at[h, c, spot(s + 1, way)])

    def ring_last(h, way):
        s = half - 1
        return move(h, s, way, way, kv_buf.at[h, way, spot(s, way)], kv_buf.at[h, way, 4 * half - 2])

    def landed(h, s, way, c):
        here = kv_buf.at[h, c, spot(s, way)]
        return move(h, s - 1, way, c, here, here)

    def share(h, s, first, count):
        return send(
            kv_buf.at[h, :, pl.ds(first, count)], kv_buf.at[h, :, pl.ds(first + count, count)],
            sib_s.at[h, s], sib_r.at[h, s], sibling,
        )

    def share_own(h):
        return share(h, 0, 0, 1)

    def share_step(h, s):
        return share(h, s, 4 * s - 2, 2)

    def share_last(h):
        return share(h, half, 4 * half - 2, 1)

    group = yl * 2 + core
    cross_yh = (yh + core) % 2

    def weight_columns(block):
        return out_weight.at[:, :, pl.ds(pl.multiple_of(block * out_cols, out_cols), out_cols)]

    def weight_own():
        return pltpu.make_async_copy(weight_columns(group), out_weight_all.at[:, group], own_sem)

    def weight_sibling(slot):
        return send(
            weight_columns(yl * 2 + 1 - core), out_weight_all.at[:, slot],
            w_s.at[2], w_r.at[2], sibling,
        )

    def weight_cross(c, slot, source_core):
        return send(
            weight_columns((1 - yl) * 2 + c), out_weight_all.at[:, slot],
            w_s.at[c], w_r.at[source_core], device(x, cross_yh, z, 1 - yl, c),
        )

    def sum_num(h, j, i):
        return send(
            num_stage.at[h, j - 1, i], num_in.at[h, j - 1, i],
            sum_s.at[h, j - 1, i], sum_r.at[h, j - 1, i], along_x(nx - j),
        )

    def sum_den(h, j):
        return send(
            den.at[h, :, pl.ds(j * rows, rows)], den_in.at[h, j - 1],
            sum_s.at[h, j - 1, tiles], sum_r.at[h, j - 1, tiles], along_x(nx - j),
        )

    held_group = (1 - yl) * 2 + yh

    def hand_out(h, i, d, slot):
        return send(
            att_stage.at[h, i], att_all.at[h, i, slot],
            att_s.at[h, i, d], att_r.at[h, i, slot], device(x, core, z, d // 2, d % 2),
        )

    def compute(h, first, count, fresh):
        keys = kv_buf[h, 0, pl.ds(first, count)].reshape(count * rows, width)
        values = kv_buf[h, 1, pl.ds(first, count)].reshape(count * rows, width)
        scores = lax.dot_general(
            keys, q_buf[h].reshape(nx * rows, width), ROWS_BY_ROWS, preferred_element_type=jnp.float32
        )
        weights = jnp.exp2(scores)
        part = jnp.sum(weights.reshape(count * rows // 8, 8, nx * rows), axis=0)
        product = lax.dot_general(
            values, weights.astype(jnp.bfloat16), COLUMNS_BY_COLUMNS, preferred_element_type=jnp.float32
        )
        if fresh:
            acc[h], den[h] = product, part
        else:
            acc[h] += product
            den[h] += part

    def marked(i, shape):
        return jnp.broadcast_to(refresh[i], shape) > 0

    def normed(part, row):
        mean_square = jnp.mean(part * part, axis=-1, keepdims=True)
        return part * lax.rsqrt(mean_square + 1e-06) * row

    load_tokens.start()
    for j in range(2):
        load_kv_weight(0, j).start()
        if j == 0:
            for copy in (load_gain, load_refresh, load_stale_kv):
                copy.start()

    barrier = pltpu.get_barrier_semaphore()
    peers = [along_x(j) for j in range(1, nx)] + list(along_z)
    for other in range(1, 8):
        bits = (other // 4, (other // 2) % 2, other % 2)
        peers.append(device(x, (yh + bits[0]) % 2, z, (yl + bits[1]) % 2, (core + bits[2]) % 2))
    for peer in peers:
        pl.semaphore_signal(barrier, inc=1, device_id=peer, device_id_type=MESH)

    load_tokens.wait()
    load_kv_weight(0, 0).wait()
    for h in range(1, heads):
        for j in range(2):
            load_kv_weight(h, j).start()
    load_q_weight.start()
    load_stale_out.start()
    for copy in (load_gain, load_refresh, load_stale_kv):
        copy.wait()
    scale = math.log2(math.e) / math.sqrt(width)
    query_gain = gain[pl.ds(0, 1), :] * scale
    key_gain = gain[pl.ds(1, 1), :]

    def place(h, j, fresh):
        stale = stale_kv[:, :, h * width : (h + 1) * width].astype(jnp.float32)
        for i in range(tiles):
            span = slice(i * tile_rows, (i + 1) * tile_rows)
            kept = stale[span, j, :]
            stage[h, 1 + j, span] = jnp.where(marked(i, kept.shape), fresh[span], kept).astype(jnp.bfloat16)
        if h == 0 and j == 0:
            pl.semaphore_wait(barrier, len(peers))
        swap(h, 1 + j).start()

    def project(h, columns):
        return jnp.dot(tokens[...], kv_weight[h, :, columns], preferred_element_type=jnp.float32)

    place(0, 0, normed(project(0, slice(0, width)), key_gain))
    load_kv_weight(0, 1).wait()
    place(0, 1, project(0, slice(width, 2 * width)))
    for h in range(1, heads):
        for j in range(2):
            load_kv_weight(h, j).wait()
        fresh = project(h, slice(0, 2 * width))
        place(h, 0, normed(fresh[:, :width], key_gain))
        place(h, 1, fresh[:, width:])

    load_q_weight.wait()
    fresh = jnp.dot(tokens[...], q_weight[...], preferred_element_type=jnp.float32)
    for h in range(heads):
        stage[h, 0] = normed(fresh[:, h * width : (h + 1) * width], query_gain).astype(jnp.bfloat16)
        swap(h, 0).start()

    def distribute_kv(h, carry):
        for c in range(2):
            swap(h, 1 + c).wait_recv()
            for way in range(2):
                ring_own(h, way, c).start()
        share_own(h).start()
        return carry

    def distribute_q(h, carry):
        swap(h, 0).wait_recv()
        for j in range(1, nx):
            gather_x(h, j).start()
        return carry

    lax.fori_loop(0, heads, distribute_kv, 0)
    lax.fori_loop(0, heads, distribute_q, 0)
    weight_own().start()
    weight_sibling(group).start()
    for c in range(2):
        weight_cross(c, group, core).start()

    order = sorted(
        ((h, s) for h in range(heads) for s in range(1, half + 1)),
        key=lambda pair: (pair[0] + 2 * pair[1], pair[0]),
    )

    def look_up(i):
        h, s = order[0]
        for place, (h_there, s_there) in enumerate(order):
            h = jnp.where(i == place, h_there, h)
            s = jnp.where(i == place, s_there, s)
        return h, s

    def arrive(h, s):
        @pl.when(s < half - 1)
        def _():
            for turned in range(2):
                for way in range(2):
                    c = (way + turned) % 2
                    landed(h, s, way, c).wait_recv()
                    ring(h, s, way, c).start()

        @pl.when(s == half - 1)
        def _():
            for way in range(2):
                landed(h, s, way, way).wait_recv()
                ring_last(h, way).start()
            for way in range(2):
                landed(h, s, way, 1 - way).wait_recv()

        @pl.when(s < half)
        def _():
            share_step(h, s).start()

        @pl.when(s == half)
        def _():
            for way in range(2):
                ring_last(h, way).wait_recv()
            share_last(h).start()

    def work(h, s):
        @pl.when(s == 1)
        def _():
            for j in range(1, nx):
                gather_x(h, j).wait_recv()
            share_own(h).wait_recv()
            compute(h, 0, 2, True)

        @pl.when(s < half)
        def _():
            share_step(h, s).wait_recv()
            compute(h, 4 * s - 2, 4, False)

        @pl.when(s == half)
        def _():
            share_last(h).wait_recv()
            compute(h, 4 * half - 2, 2, False)
            for j in range(1, nx):
                sum_den(h, j).start()
            for i in range(tiles):
                for j in range(1, nx):
                    first = j * rows + i * tile_rows
                    num_stage[h, j - 1, i] = acc[h, :, first : first + tile_rows].astype(jnp.bfloat16)
                    sum_num(h, j, i).start()

    def turn(i, carry):
        @pl.when(i < len(order))
        def _():
            arrive(*look_up(i))

        @pl.when(i > 0)
        def _():
            work(*look_up(i - 1))

        return carry

    lax.fori_loop(0, len(order) + 1, turn, 0)

    def drain_early(h, carry):
        for j in range(3):
            swap(h, j).wait_send()
        for j in range(1, nx):
            gather_x(h, j).wait_send()
        for way in range(2):
            for c in range(2):
                ring_own(h, way, c).wait_send()
                for s in range(1, half - 1):
                    ring(h, s, way, c).wait_send()
            ring_last(h, way).wait_send()
        share_own(h).wait_send()
        for s in range(1, half):
            share_step(h, s).wait_send()
        share_last(h).wait_send()
        return carry

    lax.fori_loop(0, heads, drain_early, 0)
    weight_own().wait()
    weight_sibling(yl * 2 + 1 - core).wait_recv()
    weight_sibling(group).wait_send()
    for c in range(2):
        weight_cross(c, (1 - yl) * 2 + c, c).wait_recv()
        weight_cross(c, group, core).wait_send()
    load_stale_out.wait()

    def attended(h, carry):
        denominator = den[h, :, :rows]
        for j in range(1, nx):
            sum_den(h, j).wait_recv()
            denominator += den_in[h, j - 1]
        denominator = jnp.sum(denominator, axis=0, keepdims=True)
        for i in range(tiles):
            span = slice(i * tile_rows, (i + 1) * tile_rows)
            numerator = acc[h, :, span]
            for j in range(1, nx):
                sum_num(h, j, i).wait_recv()
                numerator += num_in[h, j - 1, i].astype(jnp.float32)
            result = (numerator / denominator[:, span]).astype(jnp.bfloat16)
            att_stage[h, i] = result
            for d in range(4):

                @pl.when(jnp.logical_or(yh != core, head != d))
                def _(d=d, i=i):
                    hand_out(h, i, d, held_group).start()

            @pl.when(yh == core)
            def _(i=i, result=result):
                att_all[h, i, held_group] = result

        return carry

    lax.fori_loop(0, heads, attended, 0)

    def drain_sums(h, carry):
        for j in range(1, nx):
            sum_den(h, j).wait_send()
            for i in range(tiles):
                sum_num(h, j, i).wait_send()
        return carry

    lax.fori_loop(0, heads, drain_sums, 0)

    total = [None] * tiles
    for h in range(heads):
        for i in range(tiles):
            for slot in range(4):

                @pl.when(jnp.logical_or(yh != core, held_group != slot))
                def _(h=h, i=i, slot=slot):
                    hand_out(h, i, 0, slot).wait_recv()

            part = lax.dot_general(
                att_all[h, i].reshape(4 * width, tile_rows),
                out_weight_all[h].reshape(4 * width, out_cols),
                COLUMNS_BY_COLUMNS,
                preferred_element_type=jnp.float32,
            )
            total[i] = part if h == 0 else total[i] + part
            if h == heads - 1:
                span = slice(i * tile_rows, (i + 1) * tile_rows)
                stale = stale_out[span].astype(jnp.float32)
                out[span] = jnp.where(marked(i, stale.shape), total[i], stale).astype(jnp.bfloat16)

    def drain_late(h, carry):
        for i in range(tiles):
            for d in range(4):

                @pl.when(jnp.logical_or(yh != core, head != d))
                def _(i=i, d=d):
                    hand_out(h, i, d, held_group).wait_send()

        return carry

    lax.fori_loop(0, heads, drain_late, 0)


def local(nx, nz, image_tokens, refresh, qkv_weight, norm_gain, stale_kv, out_weight, stale_out):
    rows, model_width = image_tokens.shape
    group_width = qkv_weight.shape[2]
    width = norm_gain.shape[1]
    heads = group_width // width
    half = nz // 2
    out_cols = stale_out.shape[1]
    tiles = refresh.shape[0]
    tile_rows = rows // tiles
    weight = jnp.transpose(qkv_weight, (1, 0, 2))
    bf16, f32 = jnp.bfloat16, jnp.float32
    dma = pltpu.SemaphoreType.DMA
    vmem = pl.BlockSpec(memory_space=pltpu.VMEM)
    anywhere = pl.BlockSpec(memory_space=pltpu.HBM)
    return pl.pallas_call(
        functools.partial(kernel, nx, nz),
        out_shape=pltpu.VMEM((rows, out_cols), bf16),
        in_specs=[anywhere] * 7,
        out_specs=vmem,
        scratch_shapes=[
            pltpu.VMEM(image_tokens.shape, bf16),
            pltpu.SMEM(refresh.shape, jnp.int32),
            pltpu.VMEM(norm_gain.shape, f32),
            pltpu.VMEM(stale_kv.shape, bf16),
            pltpu.VMEM(stale_out.shape, bf16),
            pltpu.VMEM((heads, model_width, 2 * width), bf16),
            pltpu.VMEM((model_width, group_width), bf16),
            pltpu.VMEM((heads, 3, rows, width), bf16),
            pltpu.VMEM((heads, 2, 4 * half, rows, width), bf16),
            pltpu.VMEM((heads, nx, rows, width), bf16),
            pltpu.VMEM((heads, width, nx * rows), f32),
            pltpu.VMEM((heads, 8, nx * rows), f32),
            pltpu.VMEM((heads, nx - 1, tiles, width, tile_rows), bf16),
            pltpu.VMEM((heads, nx - 1, tiles, width, tile_rows), bf16),
            pltpu.VMEM((heads, nx - 1, 8, rows), f32),
            pltpu.VMEM((heads, tiles, width, tile_rows), bf16),
            pltpu.VMEM((heads, tiles, 4, width, tile_rows), bf16),
            pltpu.VMEM((heads, 4, width, out_cols), bf16),
            dma((2 * heads + 6,)), dma,
            dma((heads, 3)), dma((heads, 3)),
            dma((heads, nx - 1)), dma((heads, nx - 1)),
            dma((heads, half, 2, 2)), dma((heads, half, 2, 2)),
            dma((heads, half + 1)), dma((heads, half + 1)),
            dma((3,)), dma((3,)),
            dma((heads, nx - 1, tiles + 1)), dma((heads, nx - 1, tiles + 1)),
            dma((heads, tiles, 4)), dma((heads, tiles, 4)),
        ],
        compiler_params=pltpu.CompilerParams(
            collective_id=0, has_side_effects=True, vmem_limit_bytes=56 << 20
        ),
    )(
        *(
            pltpu.with_memory_space_constraint(array, pltpu.HBM)
            for array in (
                image_tokens, refresh, weight, norm_gain, stale_kv,
                out_weight.reshape(heads, width, out_weight.shape[1]), stale_out,
            )
        )
    )


def solution(mesh, nx=4, nz=8):
    placed = (
        P("patch", None),
        P("patch"),
        P(None, None, "head"),
        P(),
        P("patch", None, "head"),
        P("head", None),
        P("patch", "head"),
    )
    return jax.shard_map(
        functools.partial(local, nx, nz),
        mesh=mesh, in_specs=placed, out_specs=P("patch", "head"), check_vma=False,
    )
```

time: 72.9 us -> 64.5 us (0.88)
  Pallas kernels: 68 us -> 63.6 us
  local copies, waits for them, and re-layouts: 4.72 us -> 0.75 us
    pallas_call x1, Pallas kernels: 68 us -> 63.6 us  [local(): pl.pallas_call(functools.partial(kernel, nx, nz), out_shape=pltpu.VMEM((r...]
    unnamed x10 -> x1, local copies, waits for them, and re-layouts: 4.5 us -> 0.75 us
where the time goes in v3:
time: 64.5 us; the launch traced here: 64.4 us
  Pallas kernels  63.6 us (99%)
  local copies, waits for them, and re-layouts  0.75 us (1%)
    pallas_call x1, Pallas kernels, local(): pl.pallas_call(functools.partial(kernel, nx, nz), out_shape=pltpu.VMEM((r...  63.6 us

profile of v3, /device:TPU:1, one launch (start us, length us, event | category | flops | bytes accessed | tf_op | source)
XLA Modules:
  0.0 64.4 jit_solution(3495512583430304420)
XLA Ops:
  0.0 63.6 %shard_map.73 = bf16[256,768]{1,0:T(8,128)(2,1)S(1)} custom-call(bf16[256,3072]{1,0:T(8,128)(2,1)} %tokens_far.1, s32[2]{0:T(128)} %refresh_far.1, bf16[3,3072,384]{2,1,0:T(8,128)(2,1)} %bitcast.2, f32[2,128]{1,0:T(2,128)} %gain_far.1, bf16[256,2,384]{2,1,0:T(2,128)(2,1)} %stale_kv_far.1, bf16[3,128,3072]{2,1,0:T(8,128)(2,1)} %bitcast.3, ...), custom_call_target="tpu_custom_call" | custom-call | tf_op jit(solution)/shard_map/pallas_call | solution.py:444
  63.6 0.7 %copy.9 = bf16[256,768]{1,0:T(8,128)(2,1)} copy(bf16[256,768]{1,0:T(8,128)(2,1)S(1)} %shard_map.73) | data formatting | bytes 786432

commit v4 on v3

--- a/solution.py
+++ b/solution.py
@@ -20,8 +20,8 @@
     tokens, refresh, gain, stale_kv, stale_out,
     kv_weight, q_weight, stage, kv_buf, q_buf, acc, den,
     num_stage, num_in, den_in, att_stage, att_all, out_weight_all,
-    load_sem, own_sem,
-    swap_s, swap_r, x_s, x_r, z_s, z_r, sib_s, sib_r, w_s, w_r, sum_s, sum_r, att_s, att_r,
+    load_sem,
+    swap_s, swap_r, x_s, x_r, z_s, z_r, sib_s, sib_r, w_s, w_r, num_s, num_r, den_s, den_r, att_s, att_r,
 ):
     heads, _, rows, width = stage.shape
     half = nz // 2
@@ -55,50 +55,60 @@
         return pltpu.make_async_copy(
             qkv_weight.at[1 + j, :, pl.ds(h * width, width)],
             kv_weight.at[h, :, pl.ds(j * width, width)],
-            load_sem.at[2 * h + j],
+            load_sem.at[0 if h == 0 else h],
         )
 
     def load(far, near, index):
-        return pltpu.make_async_copy(far, near, load_sem.at[2 * heads + index])
-
-    load_tokens = load(tokens_far, tokens, 0)
+        return pltpu.make_async_copy(far, near, load_sem.at[heads + index])
+
+    def halves(i):
+        return pl.ds(i * (tokens.shape[1] // 2), tokens.shape[1] // 2)
+
+    def load_tokens(i):
+        return load(tokens_far.at[:, halves(i)], tokens.at[:, halves(i)], 5 + i)
+
+    def load_first(i):
+        return load(
+            qkv_weight.at[1, halves(i), pl.ds(0, width)], kv_weight.at[0, halves(i), pl.ds(0, width)], 7 + i
+        )
+
     load_refresh = load(refresh_far, refresh, 1)
     load_gain = load(gain_far, gain, 2)
     load_stale_kv = load(stale_kv_far, stale_kv, 3)
     load_stale_out = load(stale_out_far, stale_out, 4)
-    load_q_weight = load(qkv_weight.at[0], q_weight, 5)
+    load_q_weight = load(qkv_weight.at[0], q_weight, 0)
 
     def swap(h, j):
         dst = q_buf.at[h, 0] if j == 0 else kv_buf.at[h, j - 1, 0]
-        return send(stage.at[h, j], dst, swap_s.at[h, j], swap_r.at[h, j], swapped)
+        return send(stage.at[h, j], dst, swap_s, swap_r.at[h, j], swapped)
 
     def gather_x(h, j):
-        return send(q_buf.at[h, 0], q_buf.at[h, j], x_s.at[h, j - 1], x_r.at[h, j - 1], along_x(j))
+        return send(q_buf.at[h, 0], q_buf.at[h, j], x_s, x_r.at[h], along_x(j))
 
     def spot(s, way):
         return 4 * s - 2 + way
 
-    def move(h, s, way, c, src, dst):
-        return send(src, dst, z_s.at[h, s, way, c], z_r.at[h, s, way, c], along_z[way])
+    def move(h, way, index, src, dst):
+        return send(src, dst, z_s, z_r.at[h, way, index], along_z[way])
 
     def ring_own(h, way, c):
-        return move(h, 0, way, c, kv_buf.at[h, c, 0], kv_buf.at[h, c, spot(1, way)])
+        return move(h, way, c, kv_buf.at[h, c, 0], kv_buf.at[h, c, spot(1, way)])
 
     def ring(h, s, way, c):
-        return move(h, s, way, c, kv_buf.at[h, c, spot(s, way)], kv_buf.at[h, c, spot(s + 1, way)])
+        return move(h, way, 2 * s + c, kv_buf.at[h, c, spot(s, way)], kv_buf.at[h, c, spot(s + 1, way)])
 
     def ring_last(h, way):
         s = half - 1
-        return move(h, s, way, way, kv_buf.at[h, way, spot(s, way)], kv_buf.at[h, way, 4 * half - 2])
+        return move(h, way, 2 * s, kv_buf.at[h, way, spot(s, way)], kv_buf.at[h, way, 4 * half - 2])
 
     def landed(h, s, way, c):
         here = kv_buf.at[h, c, spot(s, way)]
-        return move(h, s - 1, way, c, here, here)
+        return move(h, way, 2 * (s - 1) + c, here, here)
 
     def share(h, s, first, count):
         return send(
             kv_buf.at[h, :, pl.ds(first, count)], kv_buf.at[h, :, pl.ds(first + count, count)],
-            sib_s.at[h, s], sib_r.at[h, s], sibling,
+            sib_s, sib_r.at[h, s], sibling,
         )
 
     def share_own(h):
@@ -117,30 +127,30 @@
         return out_weight.at[:, :, pl.ds(pl.multiple_of(block * out_cols, out_cols), out_cols)]
 
     def weight_own():
-        return pltpu.make_async_copy(weight_columns(group), out_weight_all.at[:, group], own_sem)
+        return pltpu.make_async_copy(weight_columns(group), out_weight_all.at[:, group], w_r)
 
     def weight_sibling(slot):
         return send(
             weight_columns(yl * 2 + 1 - core), out_weight_all.at[:, slot],
-            w_s.at[2], w_r.at[2], sibling,
-        )
-
-    def weight_cross(c, slot, source_core):
+            w_s, w_r, sibling,
+        )
+
+    def weight_cross(c, slot):
         return send(
             weight_columns((1 - yl) * 2 + c), out_weight_all.at[:, slot],
-            w_s.at[c], w_r.at[source_core], device(x, cross_yh, z, 1 - yl, c),
+            w_s, w_r, device(x, cross_yh, z, 1 - yl, c),
         )
 
     def sum_num(h, j, i):
         return send(
             num_stage.at[h, j - 1, i], num_in.at[h, j - 1, i],
-            sum_s.at[h, j - 1, i], sum_r.at[h, j - 1, i], along_x(nx - j),
+            num_s, num_r.at[h, i], along_x(nx - j),
         )
 
     def sum_den(h, j):
         return send(
             den.at[h, :, pl.ds(j * rows, rows)], den_in.at[h, j - 1],
-            sum_s.at[h, j - 1, tiles], sum_r.at[h, j - 1, tiles], along_x(nx - j),
+            den_s, den_r.at[h], along_x(nx - j),
         )
 
     held_group = (1 - yl) * 2 + yh
@@ -148,8 +158,17 @@
     def hand_out(h, i, d, slot):
         return send(
             att_stage.at[h, i], att_all.at[h, i, slot],
-            att_s.at[h, i, d], att_r.at[h, i, slot], device(x, core, z, d // 2, d % 2),
-        )
+            att_s, att_r.at[h, i], device(x, core, z, d // 2, d % 2),
+        )
+
+    def keep(h, i):
+        return pltpu.make_async_copy(att_stage.at[h, i], att_all.at[h, i, held_group], att_r.at[h, i])
+
+    def arrived(ref, sem):
+        pltpu.make_async_copy(ref, ref, sem).wait()
+
+    def left(ref, sem):
+        send(ref, ref, sem, sib_r.at[0, 0], sibling).wait_send()
 
     def compute(h, first, count, fresh):
         keys = kv_buf[h, 0, pl.ds(first, count)].reshape(count * rows, width)
@@ -175,12 +194,12 @@
         mean_square = jnp.mean(part * part, axis=-1, keepdims=True)
         return part * lax.rsqrt(mean_square + 1e-06) * row
 
-    load_tokens.start()
-    for j in range(2):
-        load_kv_weight(0, j).start()
-        if j == 0:
-            for copy in (load_gain, load_refresh, load_stale_kv):
-                copy.start()
+    for copy in (load_stale_kv, load_gain, load_refresh):
+        copy.start()
+    for i in range(2):
+        load_tokens(i).start()
+        load_first(i).start()
+    load_kv_weight(0, 1).start()
 
     barrier = pltpu.get_barrier_semaphore()
     peers = [along_x(j) for j in range(1, nx)] + list(along_z)
@@ -190,25 +209,20 @@
     for peer in peers:
         pl.semaphore_signal(barrier, inc=1, device_id=peer, device_id_type=MESH)
 
-    load_tokens.wait()
-    load_kv_weight(0, 0).wait()
-    for h in range(1, heads):
-        for j in range(2):
-            load_kv_weight(h, j).start()
-    load_q_weight.start()
-    load_stale_out.start()
-    for copy in (load_gain, load_refresh, load_stale_kv):
+    for copy in (load_stale_kv, load_gain, load_refresh):
         copy.wait()
     scale = math.log2(math.e) / math.sqrt(width)
     query_gain = gain[pl.ds(0, 1), :] * scale
     key_gain = gain[pl.ds(1, 1), :]
 
-    def place(h, j, fresh):
-        stale = stale_kv[:, :, h * width : (h + 1) * width].astype(jnp.float32)
+    def kept(h):
+        return stale_kv[:, :, h * width : (h + 1) * width].astype(jnp.float32)
+
+    def place(h, j, fresh, stale):
         for i in range(tiles):
             span = slice(i * tile_rows, (i + 1) * tile_rows)
-            kept = stale[span, j, :]
-            stage[h, 1 + j, span] = jnp.where(marked(i, kept.shape), fresh[span], kept).astype(jnp.bfloat16)
+            old = stale[span, j, :]
+            stage[h, 1 + j, span] = jnp.where(marked(i, old.shape), fresh[span], old).astype(jnp.bfloat16)
         if h == 0 and j == 0:
             pl.semaphore_wait(barrier, len(peers))
         swap(h, 1 + j).start()
@@ -216,15 +230,30 @@
     def project(h, columns):
         return jnp.dot(tokens[...], kv_weight[h, :, columns], preferred_element_type=jnp.float32)
 
-    place(0, 0, normed(project(0, slice(0, width)), key_gain))
+    stale = kept(0)
+    fresh = None
+    for i in range(2):
+        load_tokens(i).wait()
+        load_first(i).wait()
+        if i == 1:
+            for h in range(1, heads):
+                for j in range(2):
+                    load_kv_weight(h, j).start()
+            load_q_weight.start()
+            load_stale_out.start()
+        part = jnp.dot(
+            tokens[:, halves(i)], kv_weight[0, halves(i), pl.ds(0, width)], preferred_element_type=jnp.float32
+        )
+        fresh = part if i == 0 else fresh + part
+    place(0, 0, normed(fresh, key_gain), stale)
     load_kv_weight(0, 1).wait()
-    place(0, 1, project(0, slice(width, 2 * width)))
+    place(0, 1, project(0, slice(width, 2 * width)), stale)
     for h in range(1, heads):
-        for j in range(2):
-            load_kv_weight(h, j).wait()
+        arrived(kv_weight.at[h], load_sem.at[h])
         fresh = project(h, slice(0, 2 * width))
-        place(h, 0, normed(fresh[:, :width], key_gain))
-        place(h, 1, fresh[:, width:])
+        stale = kept(h)
+        place(h, 0, normed(fresh[:, :width], key_gain), stale)
+        place(h, 1, fresh[:, width:], stale)
 
     load_q_weight.wait()
     fresh = jnp.dot(tokens[...], q_weight[...], preferred_element_type=jnp.float32)
@@ -251,7 +280,7 @@
     weight_own().start()
     weight_sibling(group).start()
     for c in range(2):
-        weight_cross(c, group, core).start()
+        weight_cross(c, group).start()
 
     order = sorted(
         ((h, s) for h in range(heads) for s in range(1, half + 1)),
@@ -272,13 +301,25 @@
                 for way in range(2):
                     c = (way + turned) % 2
                     landed(h, s, way, c).wait_recv()
-                    ring(h, s, way, c).start()
+                    if turned == 0:
+                        ring(h, s, way, c).start()
+                    else:
+
+                        @pl.when(jnp.logical_or(h < heads - 1, s < half - 2))
+                        def _(way=way, c=c):
+                            ring(h, s, way, c).start()
 
         @pl.when(s == half - 1)
         def _():
             for way in range(2):
                 landed(h, s, way, way).wait_recv()
                 ring_last(h, way).start()
+
+            @pl.when(h == heads - 2)
+            def _():
+                for way in range(2):
+                    ring(heads - 1, half - 2, way, 1 - way).start()
+
             for way in range(2):
                 landed(h, s, way, 1 - way).wait_recv()
 
@@ -295,32 +336,26 @@
     def work(h, s):
         @pl.when(s == 1)
         def _():
-            for j in range(1, nx):
-                gather_x(h, j).wait_recv()
+            arrived(q_buf.at[h, pl.ds(1, nx - 1)], x_r.at[h])
             share_own(h).wait_recv()
             compute(h, 0, 2, True)
 
-        @pl.when(s < half)
-        def _():
-            share_step(h, s).wait_recv()
-            compute(h, 4 * s - 2, 4, False)
-
-        @pl.when(s == half)
-        def _():
-            share_last(h).wait_recv()
-            compute(h, 4 * half - 2, 2, False)
+        share_step(h, s).wait_recv()
+        compute(h, 4 * s - 2, 4, False)
+
+    def work_last(h):
+        share_last(h).wait_recv()
+        compute(h, 4 * half - 2, 2, False)
+        for j in range(1, nx):
+            sum_den(h, j).start()
+        for i in range(tiles):
             for j in range(1, nx):
-                sum_den(h, j).start()
-            for i in range(tiles):
-                for j in range(1, nx):
-                    first = j * rows + i * tile_rows
-                    num_stage[h, j - 1, i] = acc[h, :, first : first + tile_rows].astype(jnp.bfloat16)
-                    sum_num(h, j, i).start()
+                first = j * rows + i * tile_rows
+                num_stage[h, j - 1, i] = acc[h, :, first : first + tile_rows].astype(jnp.bfloat16)
+                sum_num(h, j, i).start()
 
     def turn(i, carry):
-        @pl.when(i < len(order))
-        def _():
-            arrive(*look_up(i))
+        arrive(*look_up(i))
 
         @pl.when(i > 0)
         def _():
@@ -328,45 +363,51 @@
 
         return carry
 
-    lax.fori_loop(0, len(order) + 1, turn, 0)
-
-    def drain_early(h, carry):
-        for j in range(3):
-            swap(h, j).wait_send()
-        for j in range(1, nx):
-            gather_x(h, j).wait_send()
-        for way in range(2):
-            for c in range(2):
-                ring_own(h, way, c).wait_send()
-                for s in range(1, half - 1):
-                    ring(h, s, way, c).wait_send()
-            ring_last(h, way).wait_send()
-        share_own(h).wait_send()
-        for s in range(1, half):
-            share_step(h, s).wait_send()
-        share_last(h).wait_send()
+    lax.fori_loop(0, len(order) - 3, turn, 0)
+    last = heads - 1
+    for way in range(2):
+        landed(last, half - 1, way, way).wait_recv()
+        ring_last(last, way).start()
+
+    def close(i, carry):
+        h = heads - 3 + i
+
+        @pl.when(i == 1)
+        def _():
+            for way in range(2):
+                landed(last, half - 1, way, 1 - way).wait_recv()
+            share_step(last, half - 1).start()
+
+        @pl.when(i == 2)
+        def _():
+            work(last, half - 1)
+
+        work_last(h)
+
+        @pl.when(i < 2)
+        def _():
+            for way in range(2):
+                ring_last(h + 1, way).wait_recv()
+            share_last(h + 1).start()
+
         return carry
 
-    lax.fori_loop(0, heads, drain_early, 0)
-    weight_own().wait()
-    weight_sibling(yl * 2 + 1 - core).wait_recv()
-    weight_sibling(group).wait_send()
-    for c in range(2):
-        weight_cross(c, (1 - yl) * 2 + c, c).wait_recv()
-        weight_cross(c, group, core).wait_send()
+    lax.fori_loop(0, 3, close, 0)
+
+    arrived(out_weight_all, w_r)
     load_stale_out.wait()
 
     def attended(h, carry):
         denominator = den[h, :, :rows]
+        arrived(den_in.at[h], den_r.at[h])
         for j in range(1, nx):
-            sum_den(h, j).wait_recv()
             denominator += den_in[h, j - 1]
         denominator = jnp.sum(denominator, axis=0, keepdims=True)
         for i in range(tiles):
             span = slice(i * tile_rows, (i + 1) * tile_rows)
             numerator = acc[h, :, span]
+            arrived(num_in.at[h, :, i], num_r.at[h, i])
             for j in range(1, nx):
-                sum_num(h, j, i).wait_recv()
                 numerator += num_in[h, j - 1, i].astype(jnp.float32)
             result = (numerator / denominator[:, span]).astype(jnp.bfloat16)
             att_stage[h, i] = result
@@ -377,31 +418,17 @@
                     hand_out(h, i, d, held_group).start()
 
             @pl.when(yh == core)
-            def _(i=i, result=result):
-                att_all[h, i, held_group] = result
+            def _(i=i):
+                keep(h, i).start()
 
         return carry
 
     lax.fori_loop(0, heads, attended, 0)
-
-    def drain_sums(h, carry):
-        for j in range(1, nx):
-            sum_den(h, j).wait_send()
-            for i in range(tiles):
-                sum_num(h, j, i).wait_send()
-        return carry
-
-    lax.fori_loop(0, heads, drain_sums, 0)
 
     total = [None] * tiles
     for h in range(heads):
         for i in range(tiles):
-            for slot in range(4):
-
-                @pl.when(jnp.logical_or(yh != core, held_group != slot))
-                def _(h=h, i=i, slot=slot):
-                    hand_out(h, i, 0, slot).wait_recv()
-
+            arrived(att_all.at[h, i], att_r.at[h, i])
             part = lax.dot_general(
                 att_all[h, i].reshape(4 * width, tile_rows),
                 out_weight_all[h].reshape(4 * width, out_cols),
@@ -414,17 +441,21 @@
                 stale = stale_out[span].astype(jnp.float32)
                 out[span] = jnp.where(marked(i, stale.shape), total[i], stale).astype(jnp.bfloat16)
 
-    def drain_late(h, carry):
-        for i in range(tiles):
-            for d in range(4):
-
-                @pl.when(jnp.logical_or(yh != core, head != d))
-                def _(i=i, d=d):
-                    hand_out(h, i, d, held_group).wait_send()
-
-        return carry
-
-    lax.fori_loop(0, heads, drain_late, 0)
+    left(stage, swap_s)
+    left(q_buf.at[:, pl.ds(0, nx - 1)], x_s)
+    left(kv_buf.at[:, :, pl.ds(0, 2 * half - 1)], z_s)
+    left(kv_buf.at[:, :, pl.ds(0, 2 * half)], sib_s)
+    left(out_weight_all.at[:, pl.ds(0, 3)], w_s)
+    left(num_stage, num_s)
+    left(den_in, den_s)
+
+    @pl.when(yh == core)
+    def _():
+        left(att_all.at[:, :, pl.ds(0, 3)], att_s)
+
+    @pl.when(yh != core)
+    def _():
+        left(att_all, att_s)
 
 
 def local(nx, nz, image_tokens, refresh, qkv_weight, norm_gain, stale_kv, out_weight, stale_out):
@@ -465,14 +496,15 @@
             pltpu.VMEM((heads, tiles, width, tile_rows), bf16),
             pltpu.VMEM((heads, tiles, 4, width, tile_rows), bf16),
             pltpu.VMEM((heads, 4, width, out_cols), bf16),
-            dma((2 * heads + 6,)), dma,
-            dma((heads, 3)), dma((heads, 3)),
-            dma((heads, nx - 1)), dma((heads, nx - 1)),
-            dma((heads, half, 2, 2)), dma((heads, half, 2, 2)),
-            dma((heads, half + 1)), dma((heads, half + 1)),
-            dma((3,)), dma((3,)),
-            dma((heads, nx - 1, tiles + 1)), dma((heads, nx - 1, tiles + 1)),
-            dma((heads, tiles, 4)), dma((heads, tiles, 4)),
+            dma((heads + 9,)),
+            dma, dma((heads, 3)),
+            dma, dma((heads,)),
+            dma, dma((heads, 2, 2 * half - 1)),
+            dma, dma((heads, half + 1)),
+            dma, dma,
+            dma, dma((heads, tiles)),
+            dma, dma((heads,)),
+            dma, dma((heads, tiles)),
         ],
         compiler_params=pltpu.CompilerParams(
             collective_id=0, has_side_effects=True, vmem_limit_bytes=56 << 20

time: 64.5 us -> 62.1 us (0.963)
  Pallas kernels: 63.6 us -> 61.3 us
    pallas_call x1, Pallas kernels: 63.6 us -> 61.3 us  [local(): pl.pallas_call(functools.partial(kernel, nx, nz), out_shape=pltpu.VMEM((r...]
where the time goes in v4:
time: 62.1 us; the launch traced here: 62 us
  Pallas kernels  61.3 us (99%)
  local copies, waits for them, and re-layouts  0.75 us (1%)
    pallas_call x1, Pallas kernels, local(): pl.pallas_call(functools.partial(kernel, nx, nz), out_shape=pltpu.VMEM((r...  61.3 us

profile of v4, /device:TPU:1, one launch (start us, length us, event | category | flops | bytes accessed | tf_op | source)
XLA Modules:
  0.0 62.0 jit_solution(13845821157130514277)
XLA Ops:
  0.0 61.3 %shard_map.73 = bf16[256,768]{1,0:T(8,128)(2,1)S(1)} custom-call(bf16[256,3072]{1,0:T(8,128)(2,1)} %tokens_far.1, s32[2]{0:T(128)} %refresh_far.1, bf16[3,3072,384]{2,1,0:T(8,128)(2,1)} %bitcast.2, f32[2,128]{1,0:T(2,128)} %gain_far.1, bf16[256,2,384]{2,1,0:T(2,128)(2,1)} %stale_kv_far.1, bf16[3,128,3072]{2,1,0:T(8,128)(2,1)} %bitcast.3, ...), custom_call_target="tpu_custom_call" | custom-call | tf_op jit(solution)/shard_map/pallas_call | solution.py:475
  61.3 0.7 %copy.9 = bf16[256,768]{1,0:T(8,128)(2,1)} copy(bf16[256,768]{1,0:T(8,128)(2,1)S(1)} %shard_map.73) | data formatting | bytes 786432

commit v5 on v4

--- a/solution.py
+++ b/solution.py
@@ -32,11 +32,14 @@
     x, yh, z = patch // (2 * nz), (patch // nz) % 2, patch % nz
     yl, core = head // 2, head % 2
 
+    far_first = sorted(range(1, nx), key=lambda step: -min(step, nx - step))
+
     def device(x_to, yh_to, z_to, yl_to, core_to):
         return ((x_to * 2 + yh_to) * nz + z_to, yl_to * 2 + core_to)
 
     sibling = device(x, yh, z, yl, 1 - core)
-    swapped = device(x, core, z, 1 - yl, yh)
+    swapped = device(x, core, z, yl, yh)
+    moves = yh != core
     along_z = (
         device(x, yh, (z + 1) % nz, yl, core),
         device(x, yh, (z + nz - 1) % nz, yl, core),
@@ -153,7 +156,7 @@
             den_s, den_r.at[h], along_x(nx - j),
         )
 
-    held_group = (1 - yl) * 2 + yh
+    held_group = yl * 2 + yh
 
     def hand_out(h, i, d, slot):
         return send(
@@ -222,10 +225,27 @@
         for i in range(tiles):
             span = slice(i * tile_rows, (i + 1) * tile_rows)
             old = stale[span, j, :]
-            stage[h, 1 + j, span] = jnp.where(marked(i, old.shape), fresh[span], old).astype(jnp.bfloat16)
+            new = jnp.where(marked(i, old.shape), fresh[span], old).astype(jnp.bfloat16)
+
+            @pl.when(moves)
+            def _(span=span, new=new):
+                stage[h, 1 + j, span] = new
+
+            @pl.when(jnp.logical_not(moves))
+            def _(span=span, new=new):
+                kv_buf[h, j, 0, span] = new
+
         if h == 0 and j == 0:
             pl.semaphore_wait(barrier, len(peers))
-        swap(h, 1 + j).start()
+
+        @pl.when(moves)
+        def _():
+            swap(h, 1 + j).start()
+
+        @pl.when(jnp.logical_not(moves))
+        def _():
+            for way in range(2):
+                ring_own(h, way, j).start()
 
     def project(h, columns):
         return jnp.dot(tokens[...], kv_weight[h, :, columns], preferred_element_type=jnp.float32)
@@ -258,21 +278,37 @@
     load_q_weight.wait()
     fresh = jnp.dot(tokens[...], q_weight[...], preferred_element_type=jnp.float32)
     for h in range(heads):
-        stage[h, 0] = normed(fresh[:, h * width : (h + 1) * width], query_gain).astype(jnp.bfloat16)
-        swap(h, 0).start()
+        query = normed(fresh[:, h * width : (h + 1) * width], query_gain).astype(jnp.bfloat16)
+
+        @pl.when(moves)
+        def _(h=h, query=query):
+            stage[h, 0] = query
+            swap(h, 0).start()
+
+        @pl.when(jnp.logical_not(moves))
+        def _(h=h, query=query):
+            q_buf[h, 0] = query
+            for j in far_first:
+                gather_x(h, j).start()
 
     def distribute_kv(h, carry):
-        for c in range(2):
-            swap(h, 1 + c).wait_recv()
-            for way in range(2):
-                ring_own(h, way, c).start()
+        @pl.when(moves)
+        def _():
+            for c in range(2):
+                swap(h, 1 + c).wait_recv()
+                for way in range(2):
+                    ring_own(h, way, c).start()
+
         share_own(h).start()
         return carry
 
     def distribute_q(h, carry):
-        swap(h, 0).wait_recv()
-        for j in range(1, nx):
-            gather_x(h, j).start()
+        @pl.when(moves)
+        def _():
+            swap(h, 0).wait_recv()
+            for j in far_first:
+                gather_x(h, j).start()
+
         return carry
 
     lax.fori_loop(0, heads, distribute_kv, 0)
@@ -346,10 +382,10 @@
     def work_last(h):
         share_last(h).wait_recv()
         compute(h, 4 * half - 2, 2, False)
-        for j in range(1, nx):
+        for j in far_first:
             sum_den(h, j).start()
         for i in range(tiles):
-            for j in range(1, nx):
+            for j in far_first:
                 first = j * rows + i * tile_rows
                 num_stage[h, j - 1, i] = acc[h, :, first : first + tile_rows].astype(jnp.bfloat16)
                 sum_num(h, j, i).start()
@@ -411,7 +447,8 @@
                 numerator += num_in[h, j - 1, i].astype(jnp.float32)
             result = (numerator / denominator[:, span]).astype(jnp.bfloat16)
             att_stage[h, i] = result
-            for d in range(4):
+            for near in range(4):
+                d = (near // 2 + yl) % 2 * 2 + near % 2
 
                 @pl.when(jnp.logical_or(yh != core, head != d))
                 def _(d=d, i=i):
@@ -441,7 +478,11 @@
                 stale = stale_out[span].astype(jnp.float32)
                 out[span] = jnp.where(marked(i, stale.shape), total[i], stale).astype(jnp.bfloat16)
 
-    left(stage, swap_s)
+
+    @pl.when(moves)
+    def _():
+        left(stage, swap_s)
+
     left(q_buf.at[:, pl.ds(0, nx - 1)], x_s)
     left(kv_buf.at[:, :, pl.ds(0, 2 * half - 1)], z_s)
     left(kv_buf.at[:, :, pl.ds(0, 2 * half)], sib_s)

time: 62.1 us -> 59.5 us (0.958)
  Pallas kernels: 61.3 us -> 58.7 us
    pallas_call x1, Pallas kernels: 61.3 us -> 58.7 us  [local(): pl.pallas_call(functools.partial(kernel, nx, nz), out_shape=pltpu.VMEM((r...]
where the time goes in v5:
time: 59.5 us; the launch traced here: 59.4 us
  Pallas kernels  58.7 us (99%)
  local copies, waits for them, and re-layouts  0.75 us (1%)
    pallas_call x1, Pallas kernels, local(): pl.pallas_call(functools.partial(kernel, nx, nz), out_shape=pltpu.VMEM((r...  58.7 us

profile of v5, /device:TPU:1, one launch (start us, length us, event | category | flops | bytes accessed | tf_op | source)
XLA Modules:
  0.0 59.4 jit_solution(1118111457871011498)
XLA Ops:
  0.0 58.7 %shard_map.73 = bf16[256,768]{1,0:T(8,128)(2,1)S(1)} custom-call(bf16[256,3072]{1,0:T(8,128)(2,1)} %tokens_far.1, s32[2]{0:T(128)} %refresh_far.1, bf16[3,3072,384]{2,1,0:T(8,128)(2,1)} %bitcast.2, f32[2,128]{1,0:T(2,128)} %gain_far.1, bf16[256,2,384]{2,1,0:T(2,128)(2,1)} %stale_kv_far.1, bf16[3,128,3072]{2,1,0:T(8,128)(2,1)} %bitcast.3, ...), custom_call_target="tpu_custom_call" | custom-call | tf_op jit(solution)/shard_map/pallas_call | solution.py:516
  58.7 0.7 %copy.9 = bf16[256,768]{1,0:T(8,128)(2,1)} copy(bf16[256,768]{1,0:T(8,128)(2,1)S(1)} %shard_map.73) | data formatting | bytes 786432

commit v6 on v5

--- a/solution.py
+++ b/solution.py
@@ -374,10 +374,13 @@
         def _():
             arrived(q_buf.at[h, pl.ds(1, nx - 1)], x_r.at[h])
             share_own(h).wait_recv()
-            compute(h, 0, 2, True)
-
-        share_step(h, s).wait_recv()
-        compute(h, 4 * s - 2, 4, False)
+            share_step(h, s).wait_recv()
+            compute(h, 0, 6, True)
+
+        @pl.when(s > 1)
+        def _():
+            share_step(h, s).wait_recv()
+            compute(h, 4 * s - 2, 4, False)
 
     def work_last(h):
         share_last(h).wait_recv()

time: 59.5 us -> 58.5 us (0.983)
  Pallas kernels: 58.7 us -> 57.7 us
    pallas_call x1, Pallas kernels: 58.7 us -> 57.7 us  [local(): pl.pallas_call(functools.partial(kernel, nx, nz), out_shape=pltpu.VMEM((r...]
where the time goes in v6:
time: 58.5 us
  Pallas kernels  57.7 us (99%)
  local copies, waits for them, and re-layouts  0.75 us (1%)
    pallas_call x1, Pallas kernels, local(): pl.pallas_call(functools.partial(kernel, nx, nz), out_shape=pltpu.VMEM((r...  57.7 us

profile of v6, /device:TPU:1, one launch (start us, length us, event | category | flops | bytes accessed | tf_op | source)
XLA Modules:
  0.0 58.5 jit_solution(4729019993538943719)
XLA Ops:
  0.0 57.7 %shard_map.73 = bf16[256,768]{1,0:T(8,128)(2,1)S(1)} custom-call(bf16[256,3072]{1,0:T(8,128)(2,1)} %tokens_far.1, s32[2]{0:T(128)} %refresh_far.1, bf16[3,3072,384]{2,1,0:T(8,128)(2,1)} %bitcast.2, f32[2,128]{1,0:T(2,128)} %gain_far.1, bf16[256,2,384]{2,1,0:T(2,128)(2,1)} %stale_kv_far.1, bf16[3,128,3072]{2,1,0:T(8,128)(2,1)} %bitcast.3, ...), custom_call_target="tpu_custom_call" | custom-call | tf_op jit(solution)/shard_map/pallas_call | solution.py:519
  57.7 0.7 %copy.9 = bf16[256,768]{1,0:T(8,128)(2,1)} copy(bf16[256,768]{1,0:T(8,128)(2,1)S(1)} %shard_map.73) | data formatting | bytes 786432

commit v7 on v6

--- a/solution.py
+++ b/solution.py
@@ -313,10 +313,6 @@
 
     lax.fori_loop(0, heads, distribute_kv, 0)
     lax.fori_loop(0, heads, distribute_q, 0)
-    weight_own().start()
-    weight_sibling(group).start()
-    for c in range(2):
-        weight_cross(c, group).start()
 
     order = sorted(
         ((h, s) for h in range(heads) for s in range(1, half + 1)),
@@ -395,6 +391,13 @@
 
     def turn(i, carry):
         arrive(*look_up(i))
+
+        @pl.when(i == 2)
+        def _():
+            weight_own().start()
+            weight_sibling(group).start()
+            for c in range(2):
+                weight_cross(c, group).start()
 
         @pl.when(i > 0)
         def _():

time: 58.5 us -> 59.7 us (1.021)
  Pallas kernels: 57.7 us -> 58.9 us
    pallas_call x1, Pallas kernels: 57.7 us -> 58.9 us  [local(): pl.pallas_call(functools.partial(kernel, nx, nz), out_shape=pltpu.VMEM((r...]
where the time goes in v7:
time: 59.7 us; the launch traced here: 59.6 us
  Pallas kernels  58.9 us (99%)
  local copies, waits for them, and re-layouts  0.75 us (1%)
    pallas_call x1, Pallas kernels, local(): pl.pallas_call(functools.partial(kernel, nx, nz), out_shape=pltpu.VMEM((r...  58.9 us

profile of v7, /device:TPU:1, one launch (start us, length us, event | category | flops | bytes accessed | tf_op | source)
XLA Modules:
  0.0 59.6 jit_solution(1138356218313414412)
XLA Ops:
  0.0 58.9 %shard_map.73 = bf16[256,768]{1,0:T(8,128)(2,1)S(1)} custom-call(bf16[256,3072]{1,0:T(8,128)(2,1)} %tokens_far.1, s32[2]{0:T(128)} %refresh_far.1, bf16[3,3072,384]{2,1,0:T(8,128)(2,1)} %bitcast.2, f32[2,128]{1,0:T(2,128)} %gain_far.1, bf16[256,2,384]{2,1,0:T(2,128)(2,1)} %stale_kv_far.1, bf16[3,128,3072]{2,1,0:T(8,128)(2,1)} %bitcast.3, ...), custom_call_target="tpu_custom_call" | custom-call | tf_op jit(solution)/shard_map/pallas_call | solution.py:522
  58.9 0.7 %copy.9 = bf16[256,768]{1,0:T(8,128)(2,1)} copy(bf16[256,768]{1,0:T(8,128)(2,1)S(1)} %shard_map.73) | data formatting | bytes 786432
